TPU v7x, 256 devices: a whole 4x4x8 slice. The times are simulated.
256 devices in a mesh: dp: 8 (over z), expert: 32 (over x, y, core).
Axes of the slice: x: 4, y: 4, z: 8, core: 2. Of those that a mesh axis runs over, the one named last changes fastest.
Arguments:
- tokens: bfloat16 [32768, 4096], P(('dp', 'expert')), may hold values from -6 to 6
- latent_proj: bfloat16 [4096, 1024], P(('dp', 'expert')), may hold values from -0.09375 to 0.09375
- first_weight: bfloat16 [32, 1024, 1408], P('expert', 'dp'), may hold values from -0.1875 to 0.1875
- second_weight: bfloat16 [32, 1408, 1024], P('expert', 'dp'), may hold values from -0.15625 to 0.15625
- route_ids: int32 [32768, 4], P(('dp', 'expert')), may hold values from 0 to 31, all different within a row; in each aligned block of 128 rows (0 to 127, 128 to 255, ...) at most 24 rows name the same one
- gate_numer: int32 [32768, 4], P(('dp', 'expert')), may hold values from 1 to 256
- out_cotangent: bfloat16 [32768, 1024], P(('dp', 'expert')), may hold values from -6 to 6
Outputs:
- grad_tokens: bfloat16 [32768, 4096], P(('dp', 'expert'))
- first_grad: float32 [32, 1024, 1408], P('expert', 'dp')
- second_grad: float32 [32, 1408, 1024], P('expert', 'dp')
Inputs may be any that keep to these rules, and one draw needn't show every extreme that they name: `route_ids`: each row names 4 different experts; among the 128 rows of one device no expert is named by more than 24 routes.
All inputs are finite; a program needn't handle non-finite values.
Results may differ from a plain program's by a relative error of at most 0.015.
Values may be sent and summed in bfloat16 or wider, within the bound.
A program may use at most 128 MiB of HBM per device.

v0:
```python
import jax
import jax.numpy as jnp
from jax import lax
from jax.sharding import PartitionSpec as P

GATE_DEN = 256


def contract_last(left, right):
    return lax.dot_general(
        left, right, (((1,), (1,)), ((), ())), preferred_element_type=jnp.float32
    )


def contract_first(left, right):
    return lax.dot_general(
        left, right, (((0,), (0,)), ((), ())), preferred_element_type=jnp.float32
    )


def on_device(
    tokens, latent_proj, first_weight, second_weight, route_ids, gate_numer, out_cotangent
):
    experts = lax.axis_size("expert")
    tok_count, top_count = route_ids.shape
    width = latent_proj.shape[1]
    capacity = tok_count * top_count * 3 // (2 * experts)
    routes = tok_count * top_count
    slots = experts * capacity
    projection = lax.all_gather(latent_proj, ("dp", "expert"), axis=0, tiled=True)
    latent = jnp.dot(tokens, projection, preferred_element_type=jnp.float32).astype(jnp.bfloat16)
    flat_ids = route_ids.reshape(routes)
    onehot = (flat_ids[:, None] == jnp.arange(experts, dtype=jnp.int32)[None, :]).astype(jnp.int32)
    position = jnp.sum((jnp.cumsum(onehot, axis=0) - 1) * onehot, axis=1)
    target = flat_ids * capacity + position
    owner = jnp.arange(routes, dtype=jnp.int32) // top_count
    slot_owner = jnp.full((slots,), tok_count, jnp.int32).at[target].set(owner)
    gate_values = gate_numer.reshape(routes).astype(jnp.float32) / GATE_DEN
    slot_gate = jnp.zeros((slots,), jnp.float32).at[target].set(gate_values)
    blank = jnp.zeros((1, width), jnp.bfloat16)
    send_latent = jnp.concatenate([latent, blank])[slot_owner].reshape(experts, capacity, width)
    scaled = slot_gate[:, None] * jnp.concatenate([out_cotangent, blank])[slot_owner].astype(
        jnp.float32
    )
    send_cotangent = scaled.astype(jnp.bfloat16).reshape(experts, capacity, width)
    recv_latent, recv_cotangent = (
        lax.all_to_all(send_latent, "expert", split_axis=0, concat_axis=0, tiled=True),
        lax.all_to_all(send_cotangent, "expert", split_axis=0, concat_axis=0, tiled=True),
    )
    slot_rows = recv_latent.reshape(slots, width)
    slot_cot = recv_cotangent.reshape(slots, width)
    first_full, second_full = (
        lax.all_gather(first_weight, "dp", axis=1, tiled=True),
        lax.all_gather(second_weight, "dp", axis=1, tiled=True),
    )
    first_mat = first_full[0]
    second_mat = second_full[0]
    preact = jnp.dot(slot_rows, first_mat, preferred_element_type=jnp.float32)
    active = jnp.maximum(preact, 0.0)
    grad_hidden = contract_last(slot_cot, second_mat)
    grad_preact = (grad_hidden * 2.0 * active).astype(jnp.bfloat16)
    grad_latent = contract_last(grad_preact, first_mat)
    hidden = (active * active).astype(jnp.bfloat16)
    back_rows = grad_latent.astype(jnp.bfloat16).reshape(experts, capacity, width)
    returned = lax.all_to_all(back_rows, "expert", split_axis=0, concat_axis=0, tiled=True)
    first_term = contract_first(slot_rows, grad_preact)
    second_term = contract_first(hidden, slot_cot)
    first_grad, second_grad = (
        lax.psum_scatter(
            first_term[None].astype(jnp.bfloat16), "dp", scatter_dimension=1, tiled=True
        ).astype(jnp.float32),
        lax.psum_scatter(
            second_term[None].astype(jnp.bfloat16), "dp", scatter_dimension=1, tiled=True
        ).astype(jnp.float32),
    )
    route_grad = returned.reshape(slots, width)[target].astype(jnp.float32)
    token_grad = jnp.sum(route_grad.reshape(tok_count, top_count, width), axis=1).astype(
        jnp.bfloat16
    )
    grad_tokens = contract_last(token_grad, projection).astype(jnp.bfloat16)
    return (grad_tokens, first_grad, second_grad)


def solution(mesh):
    return jax.shard_map(
        on_device,
        mesh=mesh,
        in_specs=(
            P(("dp", "expert"), None),
            P(("dp", "expert"), None),
            P("expert", "dp", None),
            P("expert", "dp", None),
            P(("dp", "expert"), None),
            P(("dp", "expert"), None),
            P(("dp", "expert"), None),
        ),
        out_specs=(P(("dp", "expert"), None), P("expert", "dp", None), P("expert", "dp", None)),
        check_vma=False,
    )
```

profile of v0, /device:TPU:2, one launch (start us, length us, event | category | flops | bytes accessed | tf_op | source)
XLA Modules:
  0.0 331.3 jit_solution(12460343388851515780)
XLA Ops:
  7.2 0.0 copy-start
  7.2 0.0 all-gather.6.cloned.1.call-start
  7.2 0.7 all-gather.6.cloned.1.call-update
  7.9 0.0 all-gather.8.cloned.1.call-start
  8.0 0.7 all-gather.8.cloned.1.call-update
  8.7 0.0 all-gather.4.cloned.1.call-start
  8.7 0.7 all-gather.4.cloned.1.call-update
  9.4 0.8 copy.11
  10.2 0.1 eq.29
  10.3 0.1 eq.25
  10.4 1.2 reduce-window.6
  11.6 0.2 slice_reduce_fusion
  11.9 0.7 broadcast_multiply_fusion
  12.5 0.1 copy.10
  12.7 0.1 mul.44
  12.8 0.1 fusion.13
  12.9 2.4 scatter_custom_fusion.1
  15.4 117.2 %all-gather.6.cloned.1.call-done = bf16[4096,1024]{1,0:T(8,128)(2,1)} async-done(((bf16[16,1024]{1,0:T(8,128)(2,1)}), bf16[4096,1024]{1,0:T(8,128)(2,1)}) %all-gather.6.cloned.1.call-update) | async-done | bytes 8388624 | tf_op jit(solution)/shard_map/all_gather | solution.py:30
  132.6 0.0 copy-done
  132.6 4.6 %convolution_convert_fusion.3 = bf16[128,1024]{1,0:T(8,128)(2,1)S(1)} fusion(bf16[128,4096]{1,0:T(8,128)(2,1)S(1)} %copy-done, bf16[4096,1024]{1,0:T(8,128)(2,1)} %all-gather.6.cloned.1.call-done), kind=kOutput, calls=%fused_computation.21 | convolution fusion | flops 1073872896 | bytes 9699328 | tf_op jit(solution)/shard_map/dot_general | solution.py:31
  137.2 3.6 %gather_fusion.1 = bf16[768,1024]{1,0:T(8,128)(2,1)} fusion(bf16[129,1024]{1,0:T(8,128)(2,1)S(1)} %concatenate.7, s32[1024]{0:T(1024)S(1)} %pad_clamp_fusion.1), kind=kCustom, calls=%fused_computation.1 | custom fusion | bytes 3148800 | tf_op jit(solution)/shard_map/gather | solution.py:41
  140.9 0.0 copy-start.1
  140.9 6.6 %all-to-all-start.1 = ((bf16[32,24,1024]{2,1,0:T(8,128)(2,1)}), bf16[32,24,1024]{2,1,0:T(8,128)(2,1)}, u32[]{:S(2)}, u32[]{:S(2)}) async-start(bf16[32,24,1024]{2,1,0:T(8,128)(2,1)} %bitcast.6), calls=%async_computation.1 | async-start | bytes 3145728 | tf_op jit(solution)/shard_map/all_to_all | solution.py:47
  147.4 0.0 copy-done.1
  147.5 0.0 copy-start.2
  147.5 2.8 gather_fusion
  150.3 0.0 copy-done.2
  150.3 0.1 copy.14
  150.4 0.1 reshape.122
  150.5 2.4 scatter_custom_fusion
  153.0 0.1 mul.46
  153.1 1.5 fusion.2
  154.6 13.1 %all-to-all-done.1 = bf16[32,24,1024]{2,1,0:T(8,128)(2,1)} async-done(((bf16[32,24,1024]{2,1,0:T(8,128)(2,1)}), bf16[32,24,1024]{2,1,0:T(8,128)(2,1)}, u32[]{:S(2)}, u32[]{:S(2)}) %all-to-all-start.1) | async-done | bytes 1572896 | tf_op jit(solution)/shard_map/all_to_all | solution.py:47
  167.6 6.9 %all-to-all-start = ((bf16[32,24,1024]{2,1,0:T(8,128)(2,1)}), bf16[32,24,1024]{2,1,0:T(8,128)(2,1)S(1)}, u32[]{:S(2)}, u32[]{:S(2)}) async-start(bf16[32,24,1024]{2,1,0:T(8,128)(2,1)} %fusion.2), calls=%async_computation | async-start | bytes 3145728 | tf_op jit(solution)/shard_map/all_to_all | solution.py:48
  174.5 0.2 reduce-scatter.3.cloned.1.call-start
  174.8 0.7 all-gather.8.cloned.1.call-done
  175.4 6.9 %fusion.5 = f32[768,1408]{1,0:T(8,128)} fusion(bf16[768,1024]{1,0:T(8,128)(2,1)} %bitcast.7, bf16[1,1024,1408]{2,1,0:T(8,128)(2,1)} %all-gather.8.cloned.1.call-done), kind=kOutput, calls=%fused_computation.16 | convolution fusion | flops 2214592512 | bytes 8781824 | tf_op jit(solution)/shard_map/dot_general | solution.py:58
  182.3 12.4 %all-to-all-done = bf16[32,24,1024]{2,1,0:T(8,128)(2,1)S(1)} async-done(((bf16[32,24,1024]{2,1,0:T(8,128)(2,1)}), bf16[32,24,1024]{2,1,0:T(8,128)(2,1)S(1)}, u32[]{:S(2)}, u32[]{:S(2)}) %all-to-all-start) | async-done | bytes 1572896 | tf_op jit(solution)/shard_map/all_to_all | solution.py:48
  194.7 24.7 %all-gather.4.cloned.1.call-done = bf16[1,1408,1024]{2,1,0:T(8,128)(2,1)} async-done(((bf16[1,176,1024]{2,1,0:T(8,128)(2,1)}), bf16[1,1408,1024]{2,1,0:T(8,128)(2,1)}) %all-gather.4.cloned.1.call-update) | async-done | bytes 2883600 | tf_op jit(solution)/shard_map/all_gather | solution.py:54
  219.4 5.4 %multiply_convert_fusion.1 = bf16[768,1408]{1,0:T(8,128)(2,1)S(1)} fusion(f32[768,1408]{1,0:T(8,128)} %fusion.5, bf16[768,1024]{1,0:T(8,128)(2,1)S(1)} %bitcast.50, bf16[1,1408,1024]{2,1,0:T(8,128)(2,1)} %all-gather.4.cloned.1.call-done), kind=kOutput, calls=%fused_computation.7 | convolution fusion | flops 2218917888 | bytes 10944512 | tf_op jit(solution)/shard_map/dot_general | solution.py:10
  224.8 0.0 copy-start.3
  224.8 1.4 copy-done.3
  226.1 5.7 %fusion = bf16[1,1024,1408]{2,1,0:T(8,128)(2,1)} fusion(bf16[768,1024]{1,0:T(8,128)(2,1)} %bitcast.7, bf16[768,1408]{1,0:T(8,128)(2,1)S(1)} %multiply_convert_fusion.1), kind=kOutput, calls=%fused_computation.10 | convolution fusion | flops 2216034304 | bytes 6619136 | tf_op jit(solution)/shard_map/dot_general | solution.py:16
  231.8 0.0 reduce-scatter.3.cloned.1.call-update
  231.8 0.0 reduce-scatter.5.cloned.1.call-start
  231.9 6.2 %fusion.1 = bf16[1,1408,1024]{2,1,0:T(8,128)(2,1)} fusion(bf16[768,1024]{1,0:T(8,128)(2,1)S(1)} %bitcast.51, f32[768,1408]{1,0:T(8,128)} %fusion.5), kind=kOutput, calls=%fused_computation.11 | convolution fusion | flops 2219278336 | bytes 8781824 | tf_op jit(solution)/shard_map/dot_general | solution.py:16
  238.1 0.0 reduce-scatter.5.cloned.1.call-update
  238.1 6.3 %fusion.9 = bf16[768,1024]{1,0:T(8,128)(2,1)} fusion(bf16[768,1408]{1,0:T(8,128)(2,1)} %copy-done.3, bf16[1,1024,1408]{2,1,0:T(8,128)(2,1)} %all-gather.8.cloned.1.call-done), kind=kOutput, calls=%fused_computation.20 | convolution fusion | flops 2215378944 | bytes 6619136 | tf_op jit(solution)/shard_map/dot_general | solution.py:10
  244.4 7.4 %all-to-all-start.2 = ((bf16[32,24,1024]{2,1,0:T(8,128)(2,1)}), bf16[32,24,1024]{2,1,0:T(8,128)(2,1)S(1)}, u32[]{:S(2)}, u32[]{:S(2)}) async-start(bf16[32,24,1024]{2,1,0:T(8,128)(2,1)} %bitcast.52), calls=%async_computation.2 | async-start | bytes 3145728 | tf_op jit(solution)/shard_map/all_to_all | solution.py:65
  251.9 20.1 %all-to-all-done.2 = bf16[32,24,1024]{2,1,0:T(8,128)(2,1)S(1)} async-done(((bf16[32,24,1024]{2,1,0:T(8,128)(2,1)}), bf16[32,24,1024]{2,1,0:T(8,128)(2,1)S(1)}, u32[]{:S(2)}, u32[]{:S(2)}) %all-to-all-start.2) | async-done | bytes 1572896 | tf_op jit(solution)/shard_map/all_to_all | solution.py:65
  272.0 2.8 gather_fusion.2
  274.8 1.5 gather.14
  276.2 1.4 reduce_sum.25
  277.6 7.2 %convolution_convert_fusion = bf16[128,4096]{1,0:T(8,128)(2,1)} fusion(bf16[128,1024]{1,0:T(8,128)(2,1)S(1)} %reduce_sum.25, bf16[4096,1024]{1,0:T(8,128)(2,1)} %all-gather.6.cloned.1.call-done), kind=kOutput, calls=%fused_computation.5 | convolution fusion | flops 1074266112 | bytes 9699328 | tf_op jit(solution)/shard_map/dot_general | solution.py:10
  284.9 0.0 reduce-scatter.3.cloned.1.call-done
  284.9 1.9 convert_element_type.67
  286.8 36.1 %reduce-scatter.5.cloned.1.call-done = bf16[1,176,1024]{2,1,0:T(8,128)(2,1)} async-done(((bf16[1,1408,1024]{2,1,0:T(8,128)(2,1)}), bf16[1,176,1024]{2,1,0:T(8,128)(2,1)}) %reduce-scatter.5.cloned.1.call-update) | async-done | bytes 360464 | tf_op jit(solution)/shard_map/reduce_scatter | solution.py:72
  322.9 1.9 convert_element_type.71
  (11 shorter events, 0.1 us)
Async XLA Ops:
  7.2 125.4 %copy-start = (bf16[128,4096]{1,0:T(8,128)(2,1)S(1)}, bf16[128,4096]{1,0:T(8,128)(2,1)}, u32[]{:S(2)}) copy-start(bf16[128,4096]{1,0:T(8,128)(2,1)} %param.7) | copy-start | bytes 3145732
  7.2 125.4 %all-gather.6.cloned.1.call-start = ((), (), s32[]{:S(2)}) async-start(), calls=%async_computation.6 | async-start | bytes 8421376 | tf_op jit(solution)/shard_map/all_gather | solution.py:30
  7.9 167.5 %all-gather.8.cloned.1.call-start = ((), (), s32[]{:S(2)}) async-start(), calls=%async_computation.7 | async-start | bytes 3244032 | tf_op jit(solution)/shard_map/all_gather | solution.py:53
  8.7 210.7 %all-gather.4.cloned.1.call-start = ((), (), s32[]{:S(2)}) async-start(), calls=%async_computation.5 | async-start | bytes 3244032 | tf_op jit(solution)/shard_map/all_gather | solution.py:54
  140.9 6.6 %copy-start.1 = (bf16[128,1024]{1,0:T(8,128)(2,1)S(1)}, bf16[128,1024]{1,0:T(8,128)(2,1)}, u32[]{:S(2)}) copy-start(bf16[128,1024]{1,0:T(8,128)(2,1)} %param.13) | copy-start | bytes 786436
  140.9 26.8 %all-to-all-start.1 = ((bf16[32,24,1024]{2,1,0:T(8,128)(2,1)}), bf16[32,24,1024]{2,1,0:T(8,128)(2,1)}, u32[]{:S(2)}, u32[]{:S(2)}) async-start(bf16[32,24,1024]{2,1,0:T(8,128)(2,1)} %bitcast.6), calls=%async_computation.1 | async-start | bytes 3145728 | tf_op jit(solution)/shard_map/all_to_all | solution.py:47
  147.5 2.8 copy-start.2
  167.6 27.1 %all-to-all-start = ((bf16[32,24,1024]{2,1,0:T(8,128)(2,1)}), bf16[32,24,1024]{2,1,0:T(8,128)(2,1)S(1)}, u32[]{:S(2)}, u32[]{:S(2)}) async-start(bf16[32,24,1024]{2,1,0:T(8,128)(2,1)} %fusion.2), calls=%async_computation | async-start | bytes 3145728 | tf_op jit(solution)/shard_map/all_to_all | solution.py:48
  174.5 110.4 %reduce-scatter.3.cloned.1.call-start = ((), (), s32[]{:S(2)}) async-start(), calls=%async_computation.8 | async-start | bytes 3244032 | tf_op jit(solution)/shard_map/reduce_scatter | solution.py:69
  224.8 1.4 copy-start.3
  231.8 91.1 %reduce-scatter.5.cloned.1.call-start = ((), (), s32[]{:S(2)}) async-start(), calls=%async_computation.9 | async-start | bytes 3244032 | tf_op jit(solution)/shard_map/reduce_scatter | solution.py:72
  244.4 27.6 %all-to-all-start.2 = ((bf16[32,24,1024]{2,1,0:T(8,128)(2,1)}), bf16[32,24,1024]{2,1,0:T(8,128)(2,1)S(1)}, u32[]{:S(2)}, u32[]{:S(2)}) async-start(bf16[32,24,1024]{2,1,0:T(8,128)(2,1)} %bitcast.52), calls=%async_computation.2 | async-start | bytes 3145728 | tf_op jit(solution)/shard_map/all_to_all | solution.py:65
Sparse Core Ops, SparseCore 0:
  11.7 120.7 all-gather.5
  134.4 41.0 all-gather.7
  177.2 42.1 all-gather.3
  231.9 43.7 reduce-scatter.2
  278.1 44.7 reduce-scatter.4
where the time goes:
time: 332 us; the launch traced here: 331 us
  waiting for transfers between devices  226 us (68%)
  matrix products  42.3 us (13%)
  starting transfers between devices  21.3 us (6%)
  local copies, waits for them, and re-layouts  18.7 us (6%)
  between operations  14 us (4%)
  other arithmetic  8.72 us (3%)
    all_gather x1, waiting for transfers between devices, on_device(): lax.all_gather(latent_proj, ('dp', 'expert'), axis=0, tiled=True)  117 us
    reduce_scatter x1, waiting for transfers between devices, on_device(): lax.psum_scatter(second_term[None].astype(jnp.bfloat16), 'dp', scatter_di...  36.1 us
    all_gather x1, waiting for transfers between devices, on_device(): lax.all_gather(second_weight, 'dp', axis=1, tiled=True)  24.7 us
    all_to_all x1, waiting for transfers between devices, on_device(): lax.all_to_all(back_rows, 'expert', split_axis=0, concat_axis=0, tiled=True)  20.1 us
    dot_general x3, matrix products, contract_last(): lax.dot_general(left, right, (((1,), (1,)), ((), ())), preferred_element_...  18.9 us
    all_to_all x1, waiting for transfers between devices, on_device(): lax.all_to_all(send_latent, 'expert', split_axis=0, concat_axis=0, tiled=...  13.1 us
    all_to_all x1, waiting for transfers between devices, on_device(): lax.all_to_all(send_cotangent, 'expert', split_axis=0, concat_axis=0, til...  12.4 us
    dot_general x2, matrix products, contract_first(): lax.dot_general(left, right, (((0,), (0,)), ((), ())), preferred_element_...  11.9 us
  transfers between devices with their start and end apart: 8, of which 7 were waited for; matrix products, arithmetic and copies ran while one was open for 17% of the time, Pallas kernels for 0%

commit v1 on v0

--- a/solution.py
+++ b/solution.py
@@ -1,9 +1,19 @@
 import jax
 import jax.numpy as jnp
 from jax import lax
+from jax.experimental import pallas as pl
+from jax.experimental.pallas import tpu as pltpu
 from jax.sharding import PartitionSpec as P
 
 GATE_DEN = 256
+MESH = pl.DeviceIdType.MESH
+BF = jnp.bfloat16
+F32 = jnp.float32
+NZ = 8
+NX = 4
+NE = 32
+CAP = 24
+SLOTS = NE * CAP
 
 
 def contract_last(left, right):
@@ -16,6 +26,353 @@
     return lax.dot_general(
         left, right, (((0,), (0,)), ((), ())), preferred_element_type=jnp.float32
     )
+
+
+def enter(d, e):
+    barrier = pltpu.get_barrier_semaphore()
+
+    def greet_plane(i, carry):
+        pl.semaphore_signal(
+            barrier, inc=1, device_id=(d, lax.rem(e + i, NE)), device_id_type=MESH
+        )
+        return carry
+
+    def greet_column(i, carry):
+        pl.semaphore_signal(
+            barrier, inc=1, device_id=(lax.rem(d + i, NZ), e), device_id_type=MESH
+        )
+        return carry
+
+    lax.fori_loop(1, NE, greet_plane, 0)
+    lax.fori_loop(1, NZ, greet_column, 0)
+    pl.semaphore_wait(barrier, NE - 1 + NZ - 1)
+
+
+def gather_kernel(
+    tokens_ref,
+    proj_ref,
+    w1_ref,
+    w2_ref,
+    ids_ref,
+    gate_ref,
+    cot_ref,
+    full_ref,
+    w1_out,
+    w2_out,
+    lat_out,
+    cot_out,
+    col,
+    pick,
+    acc,
+    send_lat,
+    send_cot,
+    barrier_free,
+    zp_send,
+    zp_recv,
+    wz_send,
+    wz_recv,
+    ax_send,
+    ax_recv,
+    mate_send,
+    mate_recv,
+    lat_send_sem,
+    lat_recv_sem,
+    cot_send_sem,
+    cot_recv_sem,
+    local_sem,
+):
+    d = lax.axis_index("dp")
+    e = lax.axis_index("expert")
+    x, y, c = e // 8, (e // 2) % NX, e % 2
+    mate = (x * NX + y) * 2 + (1 - c)
+    pending = []
+
+    def remote(src, dst, ssem, rsem, dev):
+        copy = pltpu.make_async_remote_copy(
+            src_ref=src, dst_ref=dst, send_sem=ssem, recv_sem=rsem, device_id=dev, device_id_type=MESH
+        )
+        copy.start()
+        pending.append(copy)
+        return copy
+
+    def arrived(dst, rsem):
+        pltpu.make_async_remote_copy(
+            src_ref=dst, dst_ref=dst, send_sem=rsem, recv_sem=rsem, device_id=(d, e), device_id_type=MESH
+        ).wait_recv()
+
+    enter(d, e)
+
+    for i in range(1, NZ):
+        remote(proj_ref, col.at[d, e], zp_send.at[i], zp_recv.at[i], (lax.rem(d + i, NZ), e))
+    own = [pltpu.make_async_copy(proj_ref, col.at[d, e], local_sem.at[0])]
+    own[0].start()
+
+    weights = ((w1_ref, w1_out, 128), (w2_ref, w2_out, 176))
+    for k, (src, dst, rows) in enumerate(weights):
+        copy = pltpu.make_async_copy(src.at[0], dst.at[d], local_sem.at[1 + k])
+        copy.start()
+        own.append(copy)
+    right, left = lax.rem(d + 1, NZ), lax.rem(d + NZ - 1, NZ)
+
+    def halves(k, way):
+        rows = weights[k][2]
+        cut = 64 if k == 0 else 96
+        return pl.ds(0, cut) if way == 0 else pl.ds(cut, rows - cut)
+
+    def ring_send(s, k, way):
+        src, dst, rows = weights[k]
+        owner = lax.rem(d - s + NZ, NZ) if way == 0 else lax.rem(d + s, NZ)
+        to = (right, e) if way == 0 else (left, e)
+        part = halves(k, way) if s == 3 else pl.ds(0, rows)
+        source = src.at[0] if s == 0 else dst.at[owner, part]
+        remote(source, dst.at[owner, part], wz_send.at[s, k, way], wz_recv.at[s, k, way], to)
+
+    def ring_step(s, k):
+        dst, rows = weights[k][1:]
+        for way in (0, 1):
+            owner = lax.rem(d - s - 1 + NZ, NZ) if way == 0 else lax.rem(d + s + 1, NZ)
+            part = halves(k, way) if s == 3 else pl.ds(0, rows)
+            arrived(dst.at[owner, part], wz_recv.at[s, k, way])
+            if s < 3:
+                ring_send(s + 1, k, way)
+
+    for k in (0, 1):
+        for way in (0, 1):
+            ring_send(0, k, way)
+
+    slot = lax.broadcasted_iota(jnp.int32, (SLOTS, 128), 0)
+    of_expert = (slot * 2731) >> 16
+    rank_in = (slot - of_expert * CAP).astype(F32)
+    named = jnp.zeros((SLOTS, 128), F32)
+    gates = jnp.zeros((SLOTS, 128), F32)
+    for k in range(4):
+        hit = ids_ref[k : k + 1, :] == of_expert
+        named = jnp.where(hit, 1.0, named)
+        gates = jnp.where(hit, gate_ref[k : k + 1, :].astype(F32) * (1.0 / GATE_DEN), gates)
+    before = lax.broadcasted_iota(jnp.int32, (128, 128), 0) < lax.broadcasted_iota(
+        jnp.int32, (128, 128), 1
+    )
+    rank = jnp.dot(named.astype(BF), jnp.where(before, 1.0, 0.0).astype(BF), preferred_element_type=F32)
+    chosen = jnp.logical_and(named > 0.0, rank == rank_in)
+    pick[0] = jnp.where(chosen, 1.0, 0.0).astype(BF)
+    pick[1] = jnp.where(chosen, gates, 0.0).astype(BF)
+
+    def pack(which, rows_ref, out):
+        for j in range(4):
+            block = jnp.dot(
+                pick[which, 192 * j : 192 * (j + 1), :], rows_ref[...], preferred_element_type=F32
+            )
+            for i in range(8):
+                out[8 * j + i] = block[CAP * i : CAP * (i + 1), :].astype(BF)
+
+    pack(1, cot_ref, send_cot)
+
+    for i in range(1, NZ):
+        arrived(col.at[lax.rem(d - i + NZ, NZ), e], zp_recv.at[i])
+    own[0].wait()
+
+    pos = ((x, y), (y, x))
+
+    def device(h, p, q):
+        p, q = lax.rem(p + 2 * NX, NX), lax.rem(q + 2 * NX, NX)
+        return (p * NX + q) * 2 + c if h == 0 else (q * NX + p) * 2 + c
+
+    def piece(h, who, sub=None):
+        if sub is None:
+            return col.at[pl.ds(4 * h, 4), who]
+        return col.at[pl.ds(4 * h + 2 * sub, 2), who]
+
+    def share(h, who, n):
+        remote(piece(h, who), piece(h, who), mate_send.at[h, n], mate_recv.at[h, n], (d, mate))
+
+    def spread(h, axis, who, n, sub=None, way=None):
+        p, q = pos[h]
+        for w in (0, 1) if way is None else (way,):
+            step = 1 - 2 * w
+            to = device(h, p + step, q) if axis == 0 else device(h, p, q + step)
+            m = w if sub is None else 2 + w
+            remote(
+                piece(h, who, sub),
+                piece(h, who, sub),
+                ax_send.at[h, n, m],
+                ax_recv.at[h, n, m],
+                (d, to),
+            )
+
+    for h in (0, 1):
+        p, q = pos[h]
+        spread(h, 0, device(h, p, q), 0)
+    for h in (0, 1):
+        p, q = pos[h]
+        spread(h, 1, device(h, p, q), 1)
+        share(h, device(h, p, q), 0)
+    for h in (0, 1):
+        p, q = pos[h]
+        for w in (0, 1):
+            who = device(h, p - 1 + 2 * w, q)
+            arrived(piece(h, who), ax_recv.at[h, 0, w])
+            spread(h, 0, who, 0, sub=w, way=w)
+            spread(h, 1, who, 2 + w)
+            share(h, who, 1 + w)
+    for h in (0, 1):
+        p, q = pos[h]
+        who = device(h, p + 2, q)
+        for w in (0, 1):
+            arrived(piece(h, who, w), ax_recv.at[h, 0, 2 + w])
+        spread(h, 1, who, 4)
+        share(h, who, 3)
+    ring_step(0, 0)
+
+    def second_stage(n):
+        for h in (0, 1):
+            p, q = pos[h]
+            r = p + (0, -1, 1, 2)[n]
+            for w in (0, 1):
+                who = device(h, r, q - 1 + 2 * w)
+                arrived(piece(h, who), ax_recv.at[h, 1 + n, w])
+                spread(h, 1, who, 1 + n, sub=w, way=w)
+                share(h, who, 4 + 3 * n + w)
+
+    def second_stage_far(n):
+        for h in (0, 1):
+            p, q = pos[h]
+            r = p + (0, -1, 1, 2)[n]
+            who = device(h, r, q + 2)
+            for w in (0, 1):
+                arrived(piece(h, who, w), ax_recv.at[h, 1 + n, 2 + w])
+            share(h, who, 6 + 3 * n)
+
+    second_stage(0)
+    second_stage(1)
+    second_stage(2)
+    ring_step(0, 1)
+    second_stage(3)
+
+    def dispatch(buf, out, ssem, rsem):
+        def go(i, carry):
+            to = lax.rem(e + i, NE)
+            pltpu.make_async_remote_copy(
+                src_ref=buf.at[to],
+                dst_ref=out.at[e],
+                send_sem=ssem.at[i],
+                recv_sem=rsem.at[i],
+                device_id=(d, to),
+                device_id_type=MESH,
+            ).start()
+            return carry
+
+        lax.fori_loop(1, NE, go, 0)
+        copy = pltpu.make_async_copy(buf.at[e], out.at[e], rsem.at[0])
+        copy.start()
+
+    def landed(buf, out, ssem, rsem):
+        def go(i, carry):
+            copy = pltpu.make_async_remote_copy(
+                src_ref=buf.at[lax.rem(e + i, NE)],
+                dst_ref=out.at[lax.rem(e - i + NE, NE)],
+                send_sem=ssem.at[i],
+                recv_sem=rsem.at[i],
+                device_id=(d, lax.rem(e + i, NE)),
+                device_id_type=MESH,
+            )
+            copy.wait_send()
+            copy.wait_recv()
+            return carry
+
+        lax.fori_loop(1, NE, go, 0)
+        pltpu.make_async_copy(buf.at[e], out.at[e], rsem.at[0]).wait()
+
+    dispatch(send_cot, cot_out, cot_send_sem, cot_recv_sem)
+    for n in range(4):
+        second_stage_far(n)
+    ring_step(1, 0)
+
+    def other(h, p, q):
+        p, q = lax.rem(p + 2 * NX, NX), lax.rem(q + 2 * NX, NX)
+        return ((p * NX + q) if h == 0 else (q * NX + p)) * 2 + (1 - c)
+
+    order = [(0, 0), (-1, 0), (1, 0), (2, 0)]
+    for n in range(4):
+        r = (0, -1, 1, 2)[n]
+        order += [(r, -1), (r, 1), (r, 2)]
+    for h in (0, 1):
+        p, q = pos[h]
+        for n, (a, b) in enumerate(order):
+            arrived(piece(h, other(h, p + a, q + b)), mate_recv.at[h, n])
+
+    keep = pltpu.make_async_copy(col, full_ref, local_sem.at[3])
+    keep.start()
+    acc[...] = jnp.zeros_like(acc)
+
+    def latent_step(j, carry):
+        block = col[j].reshape(512, 1024)
+        acc[...] += jnp.dot(
+            tokens_ref[:, pl.ds(pl.multiple_of(j * 512, 512), 512)], block, preferred_element_type=F32
+        )
+        return carry
+
+    lax.fori_loop(0, NZ, latent_step, 0)
+    ring_step(1, 1)
+    latent = acc[...].astype(BF)
+    for j in range(4):
+        block = jnp.dot(pick[0, 192 * j : 192 * (j + 1), :], latent, preferred_element_type=F32)
+        for i in range(8):
+            send_lat[8 * j + i] = block[CAP * i : CAP * (i + 1), :].astype(BF)
+    dispatch(send_lat, lat_out, lat_send_sem, lat_recv_sem)
+    ring_step(2, 0)
+    ring_step(2, 1)
+    landed(send_cot, cot_out, cot_send_sem, cot_recv_sem)
+    landed(send_lat, lat_out, lat_send_sem, lat_recv_sem)
+    ring_step(3, 0)
+    ring_step(3, 1)
+    for copy in pending:
+        copy.wait_send()
+    for copy in own[1:]:
+        copy.wait()
+    keep.wait()
+
+
+def gather_all(tokens, proj, w1, w2, ids, gate, cot):
+    anywhere = pl.BlockSpec(memory_space=pl.ANY)
+    vmem = pl.BlockSpec(memory_space=pltpu.VMEM)
+    dma = pltpu.SemaphoreType.DMA
+    return pl.pallas_call(
+        gather_kernel,
+        out_shape=(
+            jax.ShapeDtypeStruct((NZ, NE, 16, 1024), BF),
+            jax.ShapeDtypeStruct((NZ, 128, 1408), BF),
+            jax.ShapeDtypeStruct((NZ, 176, 1024), BF),
+            jax.ShapeDtypeStruct((NE, CAP, 1024), BF),
+            jax.ShapeDtypeStruct((NE, CAP, 1024), BF),
+        ),
+        in_specs=[vmem, anywhere, anywhere, anywhere, vmem, vmem, vmem],
+        out_specs=(anywhere,) * 5,
+        scratch_shapes=[
+            pltpu.VMEM((NZ, NE, 16, 1024), BF),
+            pltpu.VMEM((2, SLOTS, 128), BF),
+            pltpu.VMEM((128, 1024), F32),
+            pltpu.VMEM((NE, CAP, 1024), BF),
+            pltpu.VMEM((NE, CAP, 1024), BF),
+            pltpu.SemaphoreType.REGULAR,
+            dma((NZ,)),
+            dma((NZ,)),
+            dma((4, 2, 2)),
+            dma((4, 2, 2)),
+            dma((2, 5, 4)),
+            dma((2, 5, 4)),
+            dma((2, 16)),
+            dma((2, 16)),
+            dma((NE,)),
+            dma((NE,)),
+            dma((NE,)),
+            dma((NE,)),
+            dma((4,)),
+        ],
+        compiler_params=pltpu.CompilerParams(
+            collective_id=0, has_side_effects=True, vmem_limit_bytes=48 * 1024 * 1024
+        ),
+        name="gather_dispatch",
+    )(tokens, proj, w1, w2, ids, gate, cot)
 
 
 def on_device(
@@ -24,37 +381,27 @@
     experts = lax.axis_size("expert")
     tok_count, top_count = route_ids.shape
     width = latent_proj.shape[1]
-    capacity = tok_count * top_count * 3 // (2 * experts)
+    capacity = CAP
     routes = tok_count * top_count
     slots = experts * capacity
-    projection = lax.all_gather(latent_proj, ("dp", "expert"), axis=0, tiled=True)
-    latent = jnp.dot(tokens, projection, preferred_element_type=jnp.float32).astype(jnp.bfloat16)
+    full, first_full, second_full, recv_latent, recv_cotangent = gather_all(
+        tokens,
+        latent_proj,
+        first_weight,
+        second_weight,
+        route_ids.T,
+        gate_numer.T,
+        out_cotangent,
+    )
+    projection = full.reshape(4096, width)
     flat_ids = route_ids.reshape(routes)
     onehot = (flat_ids[:, None] == jnp.arange(experts, dtype=jnp.int32)[None, :]).astype(jnp.int32)
     position = jnp.sum((jnp.cumsum(onehot, axis=0) - 1) * onehot, axis=1)
     target = flat_ids * capacity + position
-    owner = jnp.arange(routes, dtype=jnp.int32) // top_count
-    slot_owner = jnp.full((slots,), tok_count, jnp.int32).at[target].set(owner)
-    gate_values = gate_numer.reshape(routes).astype(jnp.float32) / GATE_DEN
-    slot_gate = jnp.zeros((slots,), jnp.float32).at[target].set(gate_values)
-    blank = jnp.zeros((1, width), jnp.bfloat16)
-    send_latent = jnp.concatenate([latent, blank])[slot_owner].reshape(experts, capacity, width)
-    scaled = slot_gate[:, None] * jnp.concatenate([out_cotangent, blank])[slot_owner].astype(
-        jnp.float32
-    )
-    send_cotangent = scaled.astype(jnp.bfloat16).reshape(experts, capacity, width)
-    recv_latent, recv_cotangent = (
-        lax.all_to_all(send_latent, "expert", split_axis=0, concat_axis=0, tiled=True),
-        lax.all_to_all(send_cotangent, "expert", split_axis=0, concat_axis=0, tiled=True),
-    )
     slot_rows = recv_latent.reshape(slots, width)
     slot_cot = recv_cotangent.reshape(slots, width)
-    first_full, second_full = (
-        lax.all_gather(first_weight, "dp", axis=1, tiled=True),
-        lax.all_gather(second_weight, "dp", axis=1, tiled=True),
-    )
-    first_mat = first_full[0]
-    second_mat = second_full[0]
+    first_mat = first_full.reshape(1024, 1408)
+    second_mat = second_full.reshape(1408, 1024)
     preact = jnp.dot(slot_rows, first_mat, preferred_element_type=jnp.float32)
     active = jnp.maximum(preact, 0.0)
     grad_hidden = contract_last(slot_cot, second_mat)

time: 332 us -> 218 us (0.66)
  waiting for transfers between devices: 226 us -> 56.7 us
  Pallas kernels: 0 us -> 92.8 us
  starting transfers between devices: 21.3 us -> 4.15 us
  matrix products: 42.3 us -> 30.4 us
  local copies, waits for them, and re-layouts: 18.7 us -> 12.7 us
    all_gather x3 -> x0, waiting for transfers between devices: 143 us -> none  [the longest x1 117 us: on_device(): lax.all_gather(latent_proj, ('dp', 'expert'), axis=0, tiled=True)]
    pallas_call x0 -> x1, Pallas kernels: none -> 92.8 us  [gather_all(): pl.pallas_call(gather_kernel, out_shape=(jax.ShapeDtypeStruct((NZ, NE, 16...]
    all_to_all x2 -> x0, waiting for transfers between devices: 25.5 us -> none  [the longest x1 13.1 us: on_device(): lax.all_to_all(send_latent, 'expert', split_axis=0, concat_axis=0, tiled=...]
    all_to_all x2 -> x0, starting transfers between devices: 13.5 us -> none  [the longest x1 6.9 us: on_device(): lax.all_to_all(send_cotangent, 'expert', split_axis=0, concat_axis=0, til...]
    unnamed x9 -> x25, local copies, waits for them, and re-layouts: 2.17 us -> 9.53 us
    gather x2 -> x0, local copies, waits for them, and re-layouts: 6.43 us -> none  [the longest x1 3.62 us: on_device(): jnp.concatenate([latent, blank])[slot_owner]]
    scatter x2 -> x0, local copies, waits for them, and re-layouts: 4.89 us -> none  [the longest x1 2.45 us: on_device(): slot_owner = jnp.full((slots,), tok_count, jnp.int32).at[target].set(owner)]
    dot_general x1 -> x0, matrix products: 4.63 us -> none  [on_device(): jnp.dot(tokens, projection, preferred_element_type=jnp.float32)]
  transfers between devices with their start and end apart: 8 -> 3, of which waited for: 7 -> 2; matrix products, arithmetic and copies ran while one was open for 17% -> 12% of each run, Pallas kernels for 0% -> 0%
where the time goes in v1:
time: 218 us; the launch traced here: 217 us
  Pallas kernels  92.8 us (43%)
  waiting for transfers between devices  56.7 us (26%)
  matrix products  30.4 us (14%)
  between operations  14.2 us (7%)
  local copies, waits for them, and re-layouts  12.7 us (6%)
  other arithmetic  6.53 us (3%)
  starting transfers between devices  4.15 us (2%)
    pallas_call x1, Pallas kernels, gather_all(): pl.pallas_call(gather_kernel, out_shape=(jax.ShapeDtypeStruct((NZ, NE, 16...  92.8 us
    reduce_scatter x1, waiting for transfers between devices, on_device(): lax.psum_scatter(second_term[None].astype(jnp.bfloat16), 'dp', scatter_di...  39.2 us
    all_to_all x1, waiting for transfers between devices, on_device(): lax.all_to_all(back_rows, 'expert', split_axis=0, concat_axis=0, tiled=True)  17.5 us
    dot_general x3, matrix products, contract_last(): lax.dot_general(left, right, (((1,), (1,)), ((), ())), preferred_element_...  15.6 us
    dot_general x2, matrix products, contract_first(): lax.dot_general(left, right, (((0,), (0,)), ((), ())), preferred_element_...  10.2 us
    unnamed x25, local copies, waits for them, and re-layouts  9.53 us
    dot_general x1, matrix products, on_device(): preact = jnp.dot(slot_rows, first_mat, preferred_element_type=jnp.float32)  4.56 us
  transfers between devices with their start and end apart: 3, of which 2 were waited for; matrix products, arithmetic and copies ran while one was open for 12% of the time, Pallas kernels for 0%

profile of v1, /device:TPU:2, one launch (start us, length us, event | category | flops | bytes accessed | tf_op | source)
XLA Modules:
  0.0 217.4 jit_solution(11628876420559132758)
XLA Ops:
  7.2 0.0 reduce-scatter.3.cloned.1.call-start
  7.2 0.0 copy-start
  7.2 1.2 copy-done
  8.4 0.0 copy-start.1
  8.4 1.0 copy-done.1
  9.4 0.0 copy-start.2
  9.4 1.0 copy-done.2
  10.4 0.0 copy-start.3
  10.4 0.9 copy-done.3
  11.4 0.0 copy-start.4
  11.4 0.8 copy-done.4
  12.1 0.0 copy-start.5
  12.1 0.7 copy-done.5
  12.8 0.0 copy-start.7
  12.8 0.7 copy-done.7
  13.5 92.8 %gather_dispatch.1 = (bf16[8,32,16,1024]{3,2,1,0:T(8,128)(2,1)}, bf16[8,128,1408]{2,1,0:T(8,128)(2,1)}, bf16[8,176,1024]{2,1,0:T(8,128)(2,1)}, bf16[32,24,1024]{...) custom-call(bf16[128,4096]{1,0:T(8,128)(2,1)S(1)} %copy-done, bf16[16,1024]{1,0:T(8,128)(2,1)S(1)} %copy-done.4, ...), custom_call_target="tpu_custom_call" | custom-call | tf_op jit(solution)/shard_map/gather_dispatch/pallas_call | solution.py:339
  106.3 0.0 copy-start.9
  106.3 4.6 %fusion.7 = f32[768,1408]{1,0:T(8,128)S(1)} fusion(bf16[768,1024]{1,0:T(8,128)(2,1)S(1)} %bitcast.45, bf16[1024,1408]{1,0:T(8,128)(2,1)} %bitcast.51), kind=kOutput, calls=%fused_computation.22 | convolution fusion | flops 2214592512 | bytes 8781824 | tf_op jit(solution)/shard_map/dot_general | solution.py:405
  110.8 0.0 copy-start.10
  110.9 0.0 copy-done.9
  110.9 2.9 %multiply_convert_fusion.1 = bf16[768,1408]{1,0:T(8,128)(2,1)S(1)} fusion(f32[768,1408]{1,0:T(8,128)S(1)} %fusion.7, bf16[768,1024]{1,0:T(8,128)(2,1)S(1)} %bitcast.43, bf16[1408,1024]{1,0:T(8,128)(2,1)S(1)} %bitcast.53), kind=kOutput, calls=%fused_computation.3 | convolution fusion | flops 2218917888 | bytes 10944512 | tf_op jit(solution)/shard_map/dot_general | solution.py:20
  113.8 0.0 copy-done.10
  113.8 0.0 copy-start.11
  113.8 1.4 copy-done.11
  115.2 4.0 %fusion = bf16[1,1024,1408]{2,1,0:T(8,128)(2,1)} fusion(bf16[768,1024]{1,0:T(8,128)(2,1)S(1)} %bitcast.46, bf16[768,1408]{1,0:T(8,128)(2,1)S(1)} %multiply_convert_fusion.1), kind=kOutput, calls=%fused_computation.6 | convolution fusion | flops 2216034304 | bytes 6619136 | tf_op jit(solution)/shard_map/dot_general | solution.py:26
  119.2 0.0 reduce-scatter.3.cloned.1.call-update
  119.2 0.0 reduce-scatter.5.cloned.1.call-start
  119.2 6.2 %fusion.1 = bf16[1,1408,1024]{2,1,0:T(8,128)(2,1)} fusion(bf16[768,1024]{1,0:T(8,128)(2,1)S(1)} %bitcast.44, f32[768,1408]{1,0:T(8,128)} %copy-done.10), kind=kOutput, calls=%fused_computation.7 | convolution fusion | flops 2219278336 | bytes 8781824 | tf_op jit(solution)/shard_map/dot_general | solution.py:26
  125.5 0.0 copy-start.8
  125.5 0.0 reduce-scatter.5.cloned.1.call-update
  125.5 1.8 copy-done.8
  127.3 5.4 %convolution_convert_fusion.3 = bf16[768,1024]{1,0:T(8,128)(2,1)} fusion(bf16[768,1408]{1,0:T(8,128)(2,1)} %copy-done.11, bf16[1024,1408]{1,0:T(8,128)(2,1)S(1)} %bitcast.52), kind=kOutput, calls=%fused_computation.9 | convolution fusion | flops 2215378944 | bytes 6619136 | tf_op jit(solution)/shard_map/dot_general | solution.py:20
  132.7 0.0 copy-start.6
  132.7 4.1 %all-to-all-start = ((bf16[32,24,1024]{2,1,0:T(8,128)(2,1)}), bf16[32,24,1024]{2,1,0:T(8,128)(2,1)S(1)}, u32[]{:S(2)}, u32[]{:S(2)}) async-start(bf16[32,24,1024]{2,1,0:T(8,128)(2,1)} %bitcast.6), calls=%async_computation | async-start | bytes 3145728 | tf_op jit(solution)/shard_map/all_to_all | solution.py:412
  136.8 0.0 copy-done.6
  136.8 0.1 copy.11
  136.9 0.1 eq.29
  137.0 0.1 eq.25
  137.1 1.2 reduce-window.6
  138.3 0.2 slice_reduce_fusion
  138.6 0.1 copy.10
  138.7 0.1 mul.36
  138.8 0.1 fusion.4
  138.9 17.5 %all-to-all-done = bf16[32,24,1024]{2,1,0:T(8,128)(2,1)S(1)} async-done(((bf16[32,24,1024]{2,1,0:T(8,128)(2,1)}), bf16[32,24,1024]{2,1,0:T(8,128)(2,1)S(1)}, u32[]{:S(2)}, u32[]{:S(2)}) %all-to-all-start) | async-done | bytes 1572896 | tf_op jit(solution)/shard_map/all_to_all | solution.py:412
  156.4 2.0 gather_fusion
  158.5 0.4 gather.6
  158.9 1.4 reduce_sum.25
  160.3 7.3 %convolution_convert_fusion = bf16[128,4096]{1,0:T(8,128)(2,1)} fusion(bf16[128,1024]{1,0:T(8,128)(2,1)S(1)} %reduce_sum.25, bf16[4096,1024]{1,0:T(8,128)(2,1)} %bitcast.48), kind=kOutput, calls=%fused_computation.1 | convolution fusion | flops 1074266112 | bytes 9699328 | tf_op jit(solution)/shard_map/dot_general | solution.py:20
  167.6 0.0 reduce-scatter.3.cloned.1.call-done
  167.6 1.9 convert_element_type.44
  169.5 39.2 %reduce-scatter.5.cloned.1.call-done = bf16[1,176,1024]{2,1,0:T(8,128)(2,1)} async-done(((bf16[1,1408,1024]{2,1,0:T(8,128)(2,1)}), bf16[1,176,1024]{2,1,0:T(8,128)(2,1)}) %reduce-scatter.5.cloned.1.call-update) | async-done | bytes 360464 | tf_op jit(solution)/shard_map/reduce_scatter | solution.py:419
  208.6 1.9 convert_element_type.48
  (6 shorter events, 0.1 us)
Async XLA Ops:
  7.2 160.4 %reduce-scatter.3.cloned.1.call-start = ((), (), s32[]{:S(2)}) async-start(), calls=%async_computation.3 | async-start | bytes 3244032 | tf_op jit(solution)/shard_map/reduce_scatter | solution.py:416
  7.2 1.2 copy-start
  8.4 1.0 copy-start.1
  9.4 1.0 copy-start.2
  10.4 0.9 copy-start.3
  11.4 0.8 copy-start.4
  12.1 0.7 copy-start.5
  12.8 0.7 copy-start.7
  106.3 4.6 %copy-start.9 = (bf16[8,176,1024]{2,1,0:T(8,128)(2,1)S(1)}, bf16[8,176,1024]{2,1,0:T(8,128)(2,1)}, u32[]{:S(2)}) copy-start(bf16[8,176,1024]{2,1,0:T(8,128)(2,1)} %get-tuple-element.9) | copy-start | bytes 8650756
  110.8 2.9 %copy-start.10 = (f32[768,1408]{1,0:T(8,128)}, f32[768,1408]{1,0:T(8,128)S(1)}, u32[]{:S(2)}) copy-start(f32[768,1408]{1,0:T(8,128)S(1)} %fusion.7) | copy-start | bytes 12976132
  113.8 1.4 copy-start.11
  119.2 89.5 %reduce-scatter.5.cloned.1.call-start = ((), (), s32[]{:S(2)}) async-start(), calls=%async_computation.4 | async-start | bytes 3244032 | tf_op jit(solution)/shard_map/reduce_scatter | solution.py:419
  125.5 1.8 copy-start.8
  132.7 4.1 %copy-start.6 = (s32[128,4]{0,1:T(4,128)S(1)}, s32[128,4]{0,1:T(4,128)}, u32[]{:S(2)}) copy-start(s32[128,4]{0,1:T(4,128)} %param.11) | copy-start | bytes 6148
  132.7 23.7 %all-to-all-start = ((bf16[32,24,1024]{2,1,0:T(8,128)(2,1)}), bf16[32,24,1024]{2,1,0:T(8,128)(2,1)S(1)}, u32[]{:S(2)}, u32[]{:S(2)}) async-start(bf16[32,24,1024]{2,1,0:T(8,128)(2,1)} %bitcast.6), calls=%async_computation | async-start | bytes 3145728 | tf_op jit(solution)/shard_map/all_to_all | solution.py:412
Sparse Core Ops, SparseCore 0:
  119.3 42.0 reduce-scatter.2
  163.9 44.6 reduce-scatter.4

commit v2 on v1

--- a/solution.py
+++ b/solution.py
@@ -22,12 +22,6 @@
     )
 
 
-def contract_first(left, right):
-    return lax.dot_general(
-        left, right, (((0,), (0,)), ((), ())), preferred_element_type=jnp.float32
-    )
-
-
 def enter(d, e):
     barrier = pltpu.get_barrier_semaphore()
 
@@ -48,25 +42,44 @@
     pl.semaphore_wait(barrier, NE - 1 + NZ - 1)
 
 
-def gather_kernel(
-    tokens_ref,
+def layer_kernel(
+    tokens_in,
     proj_ref,
     w1_ref,
     w2_ref,
     ids_ref,
     gate_ref,
-    cot_ref,
-    full_ref,
+    cot_in,
+    gt_out,
+    g1_out,
+    g2_out,
+    col,
     w1_out,
     w2_out,
     lat_out,
     cot_out,
-    col,
+    tokens_ref,
+    cot_ref,
     pick,
+    back_pick,
     acc,
     send_lat,
     send_cot,
-    barrier_free,
+    rows,
+    rows_t,
+    cots,
+    hidden_t,
+    grad_pre,
+    back_send,
+    back_recv,
+    back_rows,
+    sum1_send,
+    sum1_recv,
+    sum2_send,
+    sum2_recv,
+    gt_stage,
+    g1_stage,
+    g2_stage,
     zp_send,
     zp_recv,
     wz_send,
@@ -79,6 +92,10 @@
     lat_recv_sem,
     cot_send_sem,
     cot_recv_sem,
+    back_send_sem,
+    back_recv_sem,
+    sum_send,
+    sum_recv,
     local_sem,
 ):
     d = lax.axis_index("dp")
@@ -100,6 +117,12 @@
             src_ref=dst, dst_ref=dst, send_sem=rsem, recv_sem=rsem, device_id=(d, e), device_id_type=MESH
         ).wait_recv()
 
+    fetch = [
+        pltpu.make_async_copy(tokens_in, tokens_ref, local_sem.at[3]),
+        pltpu.make_async_copy(cot_in, cot_ref, local_sem.at[4]),
+    ]
+    for copy in fetch:
+        copy.start()
     enter(d, e)
 
     for i in range(1, NZ):
@@ -108,31 +131,35 @@
     own[0].start()
 
     weights = ((w1_ref, w1_out, 128), (w2_ref, w2_out, 176))
-    for k, (src, dst, rows) in enumerate(weights):
-        copy = pltpu.make_async_copy(src.at[0], dst.at[d], local_sem.at[1 + k])
+    def block_of(k, owner, first=0, count=None):
+        span = weights[k][2]
+        start = pl.multiple_of(owner * span + first, 16)
+        return weights[k][1].at[pl.ds(start, span if count is None else count)]
+
+    for k, (src, dst, _) in enumerate(weights):
+        copy = pltpu.make_async_copy(src.at[0], block_of(k, d), local_sem.at[1 + k])
         copy.start()
         own.append(copy)
     right, left = lax.rem(d + 1, NZ), lax.rem(d + NZ - 1, NZ)
 
+    cuts = (64, 96)
+
     def halves(k, way):
-        rows = weights[k][2]
-        cut = 64 if k == 0 else 96
-        return pl.ds(0, cut) if way == 0 else pl.ds(cut, rows - cut)
+        return (0, cuts[k]) if way == 0 else (cuts[k], weights[k][2] - cuts[k])
 
     def ring_send(s, k, way):
-        src, dst, rows = weights[k]
         owner = lax.rem(d - s + NZ, NZ) if way == 0 else lax.rem(d + s, NZ)
         to = (right, e) if way == 0 else (left, e)
-        part = halves(k, way) if s == 3 else pl.ds(0, rows)
-        source = src.at[0] if s == 0 else dst.at[owner, part]
-        remote(source, dst.at[owner, part], wz_send.at[s, k, way], wz_recv.at[s, k, way], to)
+        part = halves(k, way) if s == 3 else (0, weights[k][2])
+        target = block_of(k, owner, *part)
+        source = weights[k][0].at[0] if s == 0 else target
+        remote(source, target, wz_send.at[s, k, way], wz_recv.at[s, k, way], to)
 
     def ring_step(s, k):
-        dst, rows = weights[k][1:]
         for way in (0, 1):
             owner = lax.rem(d - s - 1 + NZ, NZ) if way == 0 else lax.rem(d + s + 1, NZ)
-            part = halves(k, way) if s == 3 else pl.ds(0, rows)
-            arrived(dst.at[owner, part], wz_recv.at[s, k, way])
+            part = halves(k, way) if s == 3 else (0, weights[k][2])
+            arrived(block_of(k, owner, *part), wz_recv.at[s, k, way])
             if s < 3:
                 ring_send(s + 1, k, way)
 
@@ -140,22 +167,26 @@
         for way in (0, 1):
             ring_send(0, k, way)
 
-    slot = lax.broadcasted_iota(jnp.int32, (SLOTS, 128), 0)
+    slot = lax.broadcasted_iota(jnp.int32, (128, SLOTS), 1)
     of_expert = (slot * 2731) >> 16
     rank_in = (slot - of_expert * CAP).astype(F32)
-    named = jnp.zeros((SLOTS, 128), F32)
-    gates = jnp.zeros((SLOTS, 128), F32)
+    named = jnp.zeros((128, SLOTS), F32)
+    gates = jnp.zeros((128, SLOTS), F32)
     for k in range(4):
-        hit = ids_ref[k : k + 1, :] == of_expert
+        hit = ids_ref[:, k : k + 1] == of_expert
         named = jnp.where(hit, 1.0, named)
-        gates = jnp.where(hit, gate_ref[k : k + 1, :].astype(F32) * (1.0 / GATE_DEN), gates)
-    before = lax.broadcasted_iota(jnp.int32, (128, 128), 0) < lax.broadcasted_iota(
-        jnp.int32, (128, 128), 1
+        gates = jnp.where(hit, gate_ref[:, k : k + 1].astype(F32) * (1.0 / GATE_DEN), gates)
+    before = lax.broadcasted_iota(jnp.int32, (128, 128), 1) < lax.broadcasted_iota(
+        jnp.int32, (128, 128), 0
     )
-    rank = jnp.dot(named.astype(BF), jnp.where(before, 1.0, 0.0).astype(BF), preferred_element_type=F32)
+    rank = jnp.dot(jnp.where(before, 1.0, 0.0).astype(BF), named.astype(BF), preferred_element_type=F32)
     chosen = jnp.logical_and(named > 0.0, rank == rank_in)
-    pick[0] = jnp.where(chosen, 1.0, 0.0).astype(BF)
-    pick[1] = jnp.where(chosen, gates, 0.0).astype(BF)
+    one_hot = jnp.where(chosen, 1.0, 0.0)
+    back_pick[...] = one_hot.astype(BF)
+    pick[0] = one_hot.T.astype(BF)
+    pick[1] = jnp.where(chosen, gates, 0.0).T.astype(BF)
+    for copy in fetch:
+        copy.wait()
 
     def pack(which, rows_ref, out):
         for j in range(4):
@@ -300,8 +331,6 @@
         for n, (a, b) in enumerate(order):
             arrived(piece(h, other(h, p + a, q + b)), mate_recv.at[h, n])
 
-    keep = pltpu.make_async_copy(col, full_ref, local_sem.at[3])
-    keep.start()
     acc[...] = jnp.zeros_like(acc)
 
     def latent_step(j, carry):
@@ -319,41 +348,193 @@
         for i in range(8):
             send_lat[8 * j + i] = block[CAP * i : CAP * (i + 1), :].astype(BF)
     dispatch(send_lat, lat_out, lat_send_sem, lat_recv_sem)
+
+    def repack(buf, out):
+        def go(j, carry):
+            pair = jnp.concatenate([buf[2 * j].astype(F32), buf[2 * j + 1].astype(F32)], axis=0)
+            out[pl.ds(pl.multiple_of(j * 48, 16), 48), :] = pair.astype(BF)
+            return carry
+
+        lax.fori_loop(0, NE // 2, go, 0)
+
     ring_step(2, 0)
+    landed(send_cot, cot_out, cot_send_sem, cot_recv_sem)
+    repack(cot_out, cots)
     ring_step(2, 1)
-    landed(send_cot, cot_out, cot_send_sem, cot_recv_sem)
     landed(send_lat, lat_out, lat_send_sem, lat_recv_sem)
+    repack(lat_out, rows)
+
+    def turn(j, carry):
+        part = pl.ds(pl.multiple_of(j * 128, 128), 128)
+        rows_t[:, part] = rows[part, :].T
+        return carry
+
+    lax.fori_loop(0, SLOTS // 128, turn, 0)
     ring_step(3, 0)
     ring_step(3, 1)
+    for copy in own[1:]:
+        copy.wait()
+
+    def hidden_tile(start, width):
+        part = pl.ds(pl.multiple_of(start, 128), width)
+        preact = jnp.dot(rows[...], w1_out[:, part], preferred_element_type=F32)
+        active = jnp.maximum(preact, 0.0)
+        hidden_t[part, :] = (active * active).astype(BF).T
+        grad_hidden = contract_last(cots[...], w2_out[part, :])
+        grad_pre[:, part] = (grad_hidden * 2.0 * active).astype(BF)
+
+    def hidden_loop(j, carry):
+        hidden_tile(j * 256, 256)
+        return carry
+
+    lax.fori_loop(0, 5, hidden_loop, 0)
+    hidden_tile(1280, 128)
+
+    sums = (
+        (sum1_send, sum1_recv, g1_stage, 128),
+        (sum2_send, sum2_recv, g2_stage, 176),
+    )
+
+    def partial_of(k, owner):
+        if k == 0:
+            block = rows_t[pl.ds(pl.multiple_of(owner * 128, 128), 128), :]
+            return jnp.dot(block, grad_pre[...], preferred_element_type=F32)
+        block = hidden_t[pl.ds(pl.multiple_of(owner * 176, 16), 176), :]
+        return jnp.dot(block, cots[...], preferred_element_type=F32)
+
+    def sum_copy(s, k, way):
+        out, inp, _, span = sums[k]
+        first, count = halves(k, way) if s == 0 else (0, span)
+        part = pl.ds(first, count)
+        return pltpu.make_async_remote_copy(
+            src_ref=out.at[s, way, part],
+            dst_ref=inp.at[s, way, part],
+            send_sem=sum_send.at[s, k, way],
+            recv_sem=sum_recv.at[s, k, way],
+            device_id=((right if way == 0 else left), e),
+            device_id_type=MESH,
+        )
+
+    def sum_send_off(s, k, way):
+        copy = sum_copy(s, k, way)
+        copy.start()
+        pending.append(copy)
+
+    def sum_step(s, k):
+        out, inp, stage, span = sums[k]
+        if s == 0:
+            block = partial_of(k, lax.rem(d + 4, NZ)).astype(BF)
+            for way in (0, 1):
+                first, count = halves(k, way)
+                out[0, way, first : first + count, :] = block[first : first + count, :]
+                sum_send_off(0, k, way)
+            return
+        if s == 4:
+            block = partial_of(k, d)
+            for way in (0, 1):
+                sum_copy(3, k, way).wait_recv()
+            stage[...] = block + inp[3, 0].astype(F32) + inp[3, 1].astype(F32)
+            return
+        for way in (0, 1):
+            owner = lax.rem(d + 4 - s, NZ) if way == 0 else lax.rem(d + 4 + s, NZ)
+            block = partial_of(k, owner)
+            sum_copy(s - 1, k, way).wait_recv()
+            if s == 1:
+                first, count = halves(k, way)
+                span_in = slice(first, first + count)
+                out[s, way] = block.astype(BF)
+                out[s, way, span_in, :] = (
+                    block[span_in, :] + inp[0, way, span_in, :].astype(F32)
+                ).astype(BF)
+            else:
+                out[s, way] = (block + inp[s - 1, way].astype(F32)).astype(BF)
+            sum_send_off(s, k, way)
+
+    sum_step(0, 1)
+    sum_step(0, 0)
+
+    def route_tile(n, carry):
+        part = pl.ds(pl.multiple_of(n * 256, 256), 256)
+        block = contract_last(grad_pre[...], w1_out[part, :])
+        for i in range(NE):
+            back_send[i, :, part] = block[CAP * i : CAP * (i + 1), :].astype(BF)
+        return carry
+
+    lax.fori_loop(0, 4, route_tile, 0)
+    dispatch(back_send, back_recv, back_send_sem, back_recv_sem)
+    sum_step(1, 1)
+    sum_step(1, 0)
+    sum_step(2, 1)
+    landed(back_send, back_recv, back_send_sem, back_recv_sem)
+    repack(back_recv, back_rows)
+    token_grad = jnp.dot(back_pick[...], back_rows[...], preferred_element_type=F32).astype(BF)
+    sum_step(2, 0)
+    sum_step(3, 1)
+    sum_step(3, 0)
+
+    def token_tile(j, carry):
+        block = contract_last(token_grad, col[j].reshape(512, 1024))
+        gt_stage[:, pl.ds(pl.multiple_of(j * 512, 512), 512)] = block.astype(BF)
+        return carry
+
+    lax.fori_loop(0, NZ, token_tile, 0)
+    leave = [pltpu.make_async_copy(gt_stage, gt_out, local_sem.at[5])]
+    leave[0].start()
+    sum_step(4, 1)
+    leave.append(pltpu.make_async_copy(g2_stage, g2_out.at[0], local_sem.at[6]))
+    leave[1].start()
+    sum_step(4, 0)
+    leave.append(pltpu.make_async_copy(g1_stage, g1_out.at[0], local_sem.at[7]))
+    leave[2].start()
     for copy in pending:
         copy.wait_send()
-    for copy in own[1:]:
+    for copy in leave:
         copy.wait()
-    keep.wait()
-
-
-def gather_all(tokens, proj, w1, w2, ids, gate, cot):
+
+
+def layer(tokens, proj, w1, w2, ids, gate, cot):
     anywhere = pl.BlockSpec(memory_space=pl.ANY)
     vmem = pl.BlockSpec(memory_space=pltpu.VMEM)
     dma = pltpu.SemaphoreType.DMA
+    slots = (NE, CAP, 1024)
+    flat = (SLOTS, 1024)
     return pl.pallas_call(
-        gather_kernel,
+        layer_kernel,
         out_shape=(
-            jax.ShapeDtypeStruct((NZ, NE, 16, 1024), BF),
-            jax.ShapeDtypeStruct((NZ, 128, 1408), BF),
-            jax.ShapeDtypeStruct((NZ, 176, 1024), BF),
-            jax.ShapeDtypeStruct((NE, CAP, 1024), BF),
-            jax.ShapeDtypeStruct((NE, CAP, 1024), BF),
+            jax.ShapeDtypeStruct((128, 4096), BF),
+            jax.ShapeDtypeStruct((1, 128, 1408), F32),
+            jax.ShapeDtypeStruct((1, 176, 1024), F32),
         ),
-        in_specs=[vmem, anywhere, anywhere, anywhere, vmem, vmem, vmem],
-        out_specs=(anywhere,) * 5,
+        in_specs=[anywhere, anywhere, anywhere, anywhere, vmem, vmem, anywhere],
+        out_specs=(anywhere,) * 3,
         scratch_shapes=[
             pltpu.VMEM((NZ, NE, 16, 1024), BF),
+            pltpu.VMEM((1024, 1408), BF),
+            pltpu.VMEM((1408, 1024), BF),
+            pltpu.VMEM(slots, BF),
+            pltpu.VMEM(slots, BF),
+            pltpu.VMEM((128, 4096), BF),
+            pltpu.VMEM((128, 1024), BF),
             pltpu.VMEM((2, SLOTS, 128), BF),
+            pltpu.VMEM((128, SLOTS), BF),
             pltpu.VMEM((128, 1024), F32),
-            pltpu.VMEM((NE, CAP, 1024), BF),
-            pltpu.VMEM((NE, CAP, 1024), BF),
-            pltpu.SemaphoreType.REGULAR,
+            pltpu.VMEM(slots, BF),
+            pltpu.VMEM(slots, BF),
+            pltpu.VMEM(flat, BF),
+            pltpu.VMEM((1024, SLOTS), BF),
+            pltpu.VMEM(flat, BF),
+            pltpu.VMEM((1408, SLOTS), BF),
+            pltpu.VMEM((SLOTS, 1408), BF),
+            pltpu.VMEM(slots, BF),
+            pltpu.VMEM(slots, BF),
+            pltpu.VMEM(flat, BF),
+            pltpu.VMEM((4, 2, 128, 1408), BF),
+            pltpu.VMEM((4, 2, 128, 1408), BF),
+            pltpu.VMEM((4, 2, 176, 1024), BF),
+            pltpu.VMEM((4, 2, 176, 1024), BF),
+            pltpu.VMEM((128, 4096), BF),
+            pltpu.VMEM((128, 1408), F32),
+            pltpu.VMEM((176, 1024), F32),
             dma((NZ,)),
             dma((NZ,)),
             dma((4, 2, 2)),
@@ -366,71 +547,22 @@
             dma((NE,)),
             dma((NE,)),
             dma((NE,)),
-            dma((4,)),
+            dma((NE,)),
+            dma((NE,)),
+            dma((4, 2, 2)),
+            dma((4, 2, 2)),
+            dma((8,)),
         ],
         compiler_params=pltpu.CompilerParams(
-            collective_id=0, has_side_effects=True, vmem_limit_bytes=48 * 1024 * 1024
+            collective_id=0, has_side_effects=True, vmem_limit_bytes=60 * 1024 * 1024
         ),
-        name="gather_dispatch",
+        name="moe_backward",
     )(tokens, proj, w1, w2, ids, gate, cot)
-
-
-def on_device(
-    tokens, latent_proj, first_weight, second_weight, route_ids, gate_numer, out_cotangent
-):
-    experts = lax.axis_size("expert")
-    tok_count, top_count = route_ids.shape
-    width = latent_proj.shape[1]
-    capacity = CAP
-    routes = tok_count * top_count
-    slots = experts * capacity
-    full, first_full, second_full, recv_latent, recv_cotangent = gather_all(
-        tokens,
-        latent_proj,
-        first_weight,
-        second_weight,
-        route_ids.T,
-        gate_numer.T,
-        out_cotangent,
-    )
-    projection = full.reshape(4096, width)
-    flat_ids = route_ids.reshape(routes)
-    onehot = (flat_ids[:, None] == jnp.arange(experts, dtype=jnp.int32)[None, :]).astype(jnp.int32)
-    position = jnp.sum((jnp.cumsum(onehot, axis=0) - 1) * onehot, axis=1)
-    target = flat_ids * capacity + position
-    slot_rows = recv_latent.reshape(slots, width)
-    slot_cot = recv_cotangent.reshape(slots, width)
-    first_mat = first_full.reshape(1024, 1408)
-    second_mat = second_full.reshape(1408, 1024)
-    preact = jnp.dot(slot_rows, first_mat, preferred_element_type=jnp.float32)
-    active = jnp.maximum(preact, 0.0)
-    grad_hidden = contract_last(slot_cot, second_mat)
-    grad_preact = (grad_hidden * 2.0 * active).astype(jnp.bfloat16)
-    grad_latent = contract_last(grad_preact, first_mat)
-    hidden = (active * active).astype(jnp.bfloat16)
-    back_rows = grad_latent.astype(jnp.bfloat16).reshape(experts, capacity, width)
-    returned = lax.all_to_all(back_rows, "expert", split_axis=0, concat_axis=0, tiled=True)
-    first_term = contract_first(slot_rows, grad_preact)
-    second_term = contract_first(hidden, slot_cot)
-    first_grad, second_grad = (
-        lax.psum_scatter(
-            first_term[None].astype(jnp.bfloat16), "dp", scatter_dimension=1, tiled=True
-        ).astype(jnp.float32),
-        lax.psum_scatter(
-            second_term[None].astype(jnp.bfloat16), "dp", scatter_dimension=1, tiled=True
-        ).astype(jnp.float32),
-    )
-    route_grad = returned.reshape(slots, width)[target].astype(jnp.float32)
-    token_grad = jnp.sum(route_grad.reshape(tok_count, top_count, width), axis=1).astype(
-        jnp.bfloat16
-    )
-    grad_tokens = contract_last(token_grad, projection).astype(jnp.bfloat16)
-    return (grad_tokens, first_grad, second_grad)
 
 
 def solution(mesh):
     return jax.shard_map(
-        on_device,
+        layer,
         mesh=mesh,
         in_specs=(
             P(("dp", "expert"), None),

time: 218 us -> 162 us (0.74)
  Pallas kernels: 92.8 us -> 153 us
  waiting for transfers between devices: 56.7 us -> 0 us
  matrix products: 30.4 us -> 0 us
  between operations: 14.2 us -> 0.66 us
  other arithmetic: 6.53 us -> 0 us
  local copies, waits for them, and re-layouts: 12.7 us -> 6.75 us
  starting transfers between devices: 4.15 us -> 0 us
    pallas_call x1, Pallas kernels: 92.8 us -> 153 us  [layer(): pl.pallas_call(layer_kernel, out_shape=(jax.ShapeDtypeStruct((128, 4096),...]
    reduce_scatter x2 -> x0, waiting for transfers between devices: 39.2 us -> none  [the longest x1 39.2 us: on_device(): lax.psum_scatter(second_term[None].astype(jnp.bfloat16), 'dp', scatter_di...]
    dot_general x6 -> x0, matrix products: 30.4 us -> none  [the longest x3 15.6 us: contract_last(): lax.dot_general(left, right, (((1,), (1,)), ((), ())), preferred_element_...]
    all_to_all x1 -> x0, waiting for transfers between devices: 17.5 us -> none  [on_device(): lax.all_to_all(back_rows, 'expert', split_axis=0, concat_axis=0, tiled=True)]
    all_to_all x1 -> x0, starting transfers between devices: 4.07 us -> none  [on_device(): lax.all_to_all(back_rows, 'expert', split_axis=0, concat_axis=0, tiled=True)]
    convert_element_type x3 -> x0, other arithmetic: 3.81 us -> none  [the longest x2 3.8 us: on_device(): first_grad, second_grad = (lax.psum_scatter(first_term[None].astype(jnp.b...]
    unnamed x25 -> x11, local copies, waits for them, and re-layouts: 9.53 us -> 6.75 us
    gather x2 -> x0, local copies, waits for them, and re-layouts: 2.48 us -> none  [on_device(): route_grad = returned.reshape(slots, width)[target].astype(jnp.float32)]
  transfers between devices with their start and end apart: 3 -> 0, of which waited for: 2 -> 0; matrix products, arithmetic and copies ran while one was open for 12% -> 0% of each run, Pallas kernels for 0% -> 0%
where the time goes in v2:
time: 162 us; the launch traced here: 161 us
  Pallas kernels  153 us (94%)
  local copies, waits for them, and re-layouts  6.75 us (4%)
    pallas_call x1, Pallas kernels, layer(): pl.pallas_call(layer_kernel, out_shape=(jax.ShapeDtypeStruct((128, 4096),...  153 us
    unnamed x11, local copies, waits for them, and re-layouts  6.75 us

profile of v2, /device:TPU:2, one launch (start us, length us, event | category | flops | bytes accessed | tf_op | source)
XLA Modules:
  0.0 160.7 jit_solution(5900516158984233069)
XLA Ops:
  0.6 0.0 copy-start.2
  0.6 1.4 copy.10.ids_ref
  2.1 0.0 copy-done.2
  2.1 0.7 copy.11.gate_ref
  2.8 153.3 %moe_backward.1 = (bf16[128,4096]{1,0:T(8,128)(2,1)}, f32[1,128,1408]{2,1,0:T(8,128)}, f32[1,176,1024]{2,1,0:T(8,128)}) custom-call(bf16[128,4096]{1,0:T(8,128)(2,1)} %tokens_in.1, bf16[16,1024]{1,0:T(8,128)(2,1)} %proj_ref.1, bf16[1,128,1408]{2,1,0:T(8,128)(2,1)} %w1_ref.1, bf16[1,176,1024]{2,1,0:T(8,128)(2,1)} %w2_ref.1, s32[128,4]{1,0:T(8,128)} %copy.10.ids_ref, ...), custom_call_target="tpu_custom_call" | custom-call | tf_op jit(solution)/shard_map/moe_backward/pallas_call | solution.py:501
  156.1 0.0 copy-start.1
  156.1 2.4 %copy.15 = bf16[128,4096]{1,0:T(8,128)(2,1)} copy(bf16[128,4096]{1,0:T(8,128)(2,1)} %get-tuple-element.6) | data formatting | bytes 2097152
  158.5 0.0 copy-done.1
  158.5 0.0 copy-start
  158.5 0.9 copy.16
  159.4 0.5 copy-done
  159.9 0.9 copy.17
Async XLA Ops:
  0.6 1.4 copy-start.2
  156.1 2.4 %copy-start.1 = (f32[1,128,1408]{2,1,0:T(8,128)S(1)}, f32[1,128,1408]{2,1,0:T(8,128)}, u32[]{:S(2)}) copy-start(f32[1,128,1408]{2,1,0:T(8,128)} %get-tuple-element.7) | copy-start | bytes 2162692
  158.5 1.4 copy-start

commit v3 on v2

--- a/solution.py
+++ b/solution.py
@@ -14,11 +14,35 @@
 NE = 32
 CAP = 24
 SLOTS = NE * CAP
+FAR_FIRST = (
+    (2, 2),
+    (2, 1),
+    (2, 3),
+    (1, 2),
+    (3, 2),
+    (2, 0),
+    (0, 2),
+    (1, 1),
+    (3, 3),
+    (1, 3),
+    (3, 1),
+    (1, 0),
+    (3, 0),
+    (0, 1),
+    (0, 3),
+)
+ORDER = [(a, b, core) for core in (0, 1) for a, b in FAR_FIRST] + [(0, 0, 1)]
 
 
 def contract_last(left, right):
     return lax.dot_general(
         left, right, (((1,), (1,)), ((), ())), preferred_element_type=jnp.float32
+    )
+
+
+def contract_first(left, right):
+    return lax.dot_general(
+        left, right, (((0,), (0,)), ((), ())), preferred_element_type=jnp.float32
     )
 
 
@@ -61,7 +85,6 @@
     tokens_ref,
     cot_ref,
     pick,
-    back_pick,
     acc,
     send_lat,
     send_cot,
@@ -69,6 +92,7 @@
     rows_t,
     cots,
     hidden_t,
+    grad_hid,
     grad_pre,
     back_send,
     back_recv,
@@ -144,49 +168,52 @@
 
     cuts = (64, 96)
 
-    def halves(k, way):
-        return (0, cuts[k]) if way == 0 else (cuts[k], weights[k][2] - cuts[k])
-
-    def ring_send(s, k, way):
+    def part_of(k, part):
+        return (0, cuts[k]) if part == 0 else (cuts[k], weights[k][2] - cuts[k])
+
+    def ring_send(s, k, part, way):
         owner = lax.rem(d - s + NZ, NZ) if way == 0 else lax.rem(d + s, NZ)
         to = (right, e) if way == 0 else (left, e)
-        part = halves(k, way) if s == 3 else (0, weights[k][2])
-        target = block_of(k, owner, *part)
-        source = weights[k][0].at[0] if s == 0 else target
-        remote(source, target, wz_send.at[s, k, way], wz_recv.at[s, k, way], to)
-
-    def ring_step(s, k):
+        first, count = part_of(k, part)
+        target = block_of(k, owner, first, count)
+        source = weights[k][0].at[0, pl.ds(first, count)] if s == 0 else target
+        remote(source, target, wz_send.at[s, k, part, way], wz_recv.at[s, k, part, way], to)
+
+    def ring_first(k, part):
         for way in (0, 1):
+            ring_send(0, k, part, way)
+
+    def ring_step(s, k, part):
+        for way in (0, 1):
+            if s == 3 and way != part:
+                continue
             owner = lax.rem(d - s - 1 + NZ, NZ) if way == 0 else lax.rem(d + s + 1, NZ)
-            part = halves(k, way) if s == 3 else (0, weights[k][2])
-            arrived(block_of(k, owner, *part), wz_recv.at[s, k, way])
-            if s < 3:
-                ring_send(s + 1, k, way)
-
-    for k in (0, 1):
-        for way in (0, 1):
-            ring_send(0, k, way)
-
-    slot = lax.broadcasted_iota(jnp.int32, (128, SLOTS), 1)
+            arrived(block_of(k, owner, *part_of(k, part)), wz_recv.at[s, k, part, way])
+            if s < 2 or (s == 2 and way == part):
+                ring_send(s + 1, k, part, way)
+
+    ring_first(1, 0)
+
+    slot = lax.broadcasted_iota(jnp.int32, (SLOTS, 128), 0)
     of_expert = (slot * 2731) >> 16
     rank_in = (slot - of_expert * CAP).astype(F32)
-    named = jnp.zeros((128, SLOTS), F32)
-    gates = jnp.zeros((128, SLOTS), F32)
+    named = jnp.zeros((SLOTS, 128), F32)
+    gates = jnp.zeros((SLOTS, 128), F32)
     for k in range(4):
-        hit = ids_ref[:, k : k + 1] == of_expert
+        hit = ids_ref[k : k + 1, :] == of_expert
         named = jnp.where(hit, 1.0, named)
-        gates = jnp.where(hit, gate_ref[:, k : k + 1].astype(F32) * (1.0 / GATE_DEN), gates)
-    before = lax.broadcasted_iota(jnp.int32, (128, 128), 1) < lax.broadcasted_iota(
-        jnp.int32, (128, 128), 0
+        gates = jnp.where(hit, gate_ref[k : k + 1, :].astype(F32) * (1.0 / GATE_DEN), gates)
+    before = lax.broadcasted_iota(jnp.int32, (128, 128), 0) < lax.broadcasted_iota(
+        jnp.int32, (128, 128), 1
     )
-    rank = jnp.dot(jnp.where(before, 1.0, 0.0).astype(BF), named.astype(BF), preferred_element_type=F32)
+    rank = jnp.dot(named.astype(BF), jnp.where(before, 1.0, 0.0).astype(BF), preferred_element_type=F32)
     chosen = jnp.logical_and(named > 0.0, rank == rank_in)
     one_hot = jnp.where(chosen, 1.0, 0.0)
-    back_pick[...] = one_hot.astype(BF)
-    pick[0] = one_hot.T.astype(BF)
-    pick[1] = jnp.where(chosen, gates, 0.0).T.astype(BF)
+    pick[0] = one_hot.astype(BF)
+    pick[1] = jnp.where(chosen, gates, 0.0).astype(BF)
     for copy in fetch:
         copy.wait()
+    ring_first(1, 1)
 
     def pack(which, rows_ref, out):
         for j in range(4):
@@ -196,7 +223,46 @@
             for i in range(8):
                 out[8 * j + i] = block[CAP * i : CAP * (i + 1), :].astype(BF)
 
+    def away(n):
+        dx, dy, dc = ORDER[n]
+        core = c if dc == 0 else 1 - c
+        to = (lax.rem(x + dx, NX) * NX + lax.rem(y + dy, NX)) * 2 + core
+        source = (lax.rem(x - dx + NX, NX) * NX + lax.rem(y - dy + NX, NX)) * 2 + core
+        return to, source
+
+    def dispatch(buf, out, ssem, rsem, lo=0, hi=NE - 1):
+        for n in range(lo, hi):
+            to = away(n)[0]
+            pltpu.make_async_remote_copy(
+                src_ref=buf.at[to],
+                dst_ref=out.at[e],
+                send_sem=ssem.at[n],
+                recv_sem=rsem.at[n],
+                device_id=(d, to),
+                device_id_type=MESH,
+            ).start()
+        if hi == NE - 1:
+            pltpu.make_async_copy(buf.at[e], out.at[e], rsem.at[hi]).start()
+
+    def landed(buf, out, ssem, rsem):
+        for n in range(NE - 1):
+            to, source = away(n)
+            copy = pltpu.make_async_remote_copy(
+                src_ref=buf.at[to],
+                dst_ref=out.at[source],
+                send_sem=ssem.at[n],
+                recv_sem=rsem.at[n],
+                device_id=(d, to),
+                device_id_type=MESH,
+            )
+            copy.wait_send()
+            copy.wait_recv()
+        pltpu.make_async_copy(buf.at[e], out.at[e], rsem.at[NE - 1]).wait()
+
     pack(1, cot_ref, send_cot)
+    ring_first(0, 0)
+    dispatch(send_cot, cot_out, cot_send_sem, cot_recv_sem, 0, 15)
+    ring_first(0, 1)
 
     for i in range(1, NZ):
         arrived(col.at[lax.rem(d - i + NZ, NZ), e], zp_recv.at[i])
@@ -237,6 +303,7 @@
         p, q = pos[h]
         spread(h, 1, device(h, p, q), 1)
         share(h, device(h, p, q), 0)
+    ring_step(0, 1, 0)
     for h in (0, 1):
         p, q = pos[h]
         for w in (0, 1):
@@ -245,6 +312,7 @@
             spread(h, 0, who, 0, sub=w, way=w)
             spread(h, 1, who, 2 + w)
             share(h, who, 1 + w)
+    ring_step(0, 1, 1)
     for h in (0, 1):
         p, q = pos[h]
         who = device(h, p + 2, q)
@@ -252,7 +320,7 @@
             arrived(piece(h, who, w), ax_recv.at[h, 0, 2 + w])
         spread(h, 1, who, 4)
         share(h, who, 3)
-    ring_step(0, 0)
+    ring_step(0, 0, 0)
 
     def second_stage(n):
         for h in (0, 1):
@@ -274,49 +342,17 @@
             share(h, who, 6 + 3 * n)
 
     second_stage(0)
+    ring_step(0, 0, 1)
     second_stage(1)
     second_stage(2)
-    ring_step(0, 1)
+    ring_step(1, 1, 0)
+    dispatch(send_cot, cot_out, cot_send_sem, cot_recv_sem, 15)
     second_stage(3)
-
-    def dispatch(buf, out, ssem, rsem):
-        def go(i, carry):
-            to = lax.rem(e + i, NE)
-            pltpu.make_async_remote_copy(
-                src_ref=buf.at[to],
-                dst_ref=out.at[e],
-                send_sem=ssem.at[i],
-                recv_sem=rsem.at[i],
-                device_id=(d, to),
-                device_id_type=MESH,
-            ).start()
-            return carry
-
-        lax.fori_loop(1, NE, go, 0)
-        copy = pltpu.make_async_copy(buf.at[e], out.at[e], rsem.at[0])
-        copy.start()
-
-    def landed(buf, out, ssem, rsem):
-        def go(i, carry):
-            copy = pltpu.make_async_remote_copy(
-                src_ref=buf.at[lax.rem(e + i, NE)],
-                dst_ref=out.at[lax.rem(e - i + NE, NE)],
-                send_sem=ssem.at[i],
-                recv_sem=rsem.at[i],
-                device_id=(d, lax.rem(e + i, NE)),
-                device_id_type=MESH,
-            )
-            copy.wait_send()
-            copy.wait_recv()
-            return carry
-
-        lax.fori_loop(1, NE, go, 0)
-        pltpu.make_async_copy(buf.at[e], out.at[e], rsem.at[0]).wait()
-
-    dispatch(send_cot, cot_out, cot_send_sem, cot_recv_sem)
+    ring_step(1, 1, 1)
+
     for n in range(4):
         second_stage_far(n)
-    ring_step(1, 0)
+    ring_step(1, 0, 0)
 
     def other(h, p, q):
         p, q = lax.rem(p + 2 * NX, NX), lax.rem(q + 2 * NX, NX)
@@ -341,7 +377,7 @@
         return carry
 
     lax.fori_loop(0, NZ, latent_step, 0)
-    ring_step(1, 1)
+    ring_step(1, 0, 1)
     latent = acc[...].astype(BF)
     for j in range(4):
         block = jnp.dot(pick[0, 192 * j : 192 * (j + 1), :], latent, preferred_element_type=F32)
@@ -357,38 +393,48 @@
 
         lax.fori_loop(0, NE // 2, go, 0)
 
-    ring_step(2, 0)
+    ring_step(2, 1, 0)
+    ring_step(2, 1, 1)
     landed(send_cot, cot_out, cot_send_sem, cot_recv_sem)
+    ring_step(2, 0, 0)
     repack(cot_out, cots)
-    ring_step(2, 1)
+    ring_step(2, 0, 1)
+    ring_step(3, 1, 0)
+    ring_step(3, 1, 1)
+    own[2].wait()
+
+    def tiles(tile):
+        def go(j, carry):
+            tile(j * 256, 256)
+            return carry
+
+        lax.fori_loop(0, 5, go, 0)
+        tile(1280, 128)
+
+    def cot_tile(start, width):
+        part = pl.ds(pl.multiple_of(start, 128), width)
+        grad_hid[:, part] = contract_last(cots[...], w2_out[part, :])
+
+    tiles(cot_tile)
+    ring_step(3, 0, 0)
+    ring_step(3, 0, 1)
+    own[1].wait()
     landed(send_lat, lat_out, lat_send_sem, lat_recv_sem)
     repack(lat_out, rows)
-
-    def turn(j, carry):
-        part = pl.ds(pl.multiple_of(j * 128, 128), 128)
-        rows_t[:, part] = rows[part, :].T
-        return carry
-
-    lax.fori_loop(0, SLOTS // 128, turn, 0)
-    ring_step(3, 0)
-    ring_step(3, 1)
-    for copy in own[1:]:
-        copy.wait()
 
     def hidden_tile(start, width):
         part = pl.ds(pl.multiple_of(start, 128), width)
         preact = jnp.dot(rows[...], w1_out[:, part], preferred_element_type=F32)
         active = jnp.maximum(preact, 0.0)
         hidden_t[part, :] = (active * active).astype(BF).T
-        grad_hidden = contract_last(cots[...], w2_out[part, :])
-        grad_pre[:, part] = (grad_hidden * 2.0 * active).astype(BF)
-
-    def hidden_loop(j, carry):
-        hidden_tile(j * 256, 256)
+        grad_pre[:, part] = (grad_hid[:, part] * 2.0 * active).astype(BF)
+
+    tiles(hidden_tile)
+
+    def turn(j, carry):
+        part = pl.ds(pl.multiple_of(j * 128, 128), 128)
+        rows_t[:, part] = rows[part, :].T
         return carry
-
-    lax.fori_loop(0, 5, hidden_loop, 0)
-    hidden_tile(1280, 128)
 
     sums = (
         (sum1_send, sum1_recv, g1_stage, 128),
@@ -402,55 +448,62 @@
         block = hidden_t[pl.ds(pl.multiple_of(owner * 176, 16), 176), :]
         return jnp.dot(block, cots[...], preferred_element_type=F32)
 
-    def sum_copy(s, k, way):
-        out, inp, _, span = sums[k]
-        first, count = halves(k, way) if s == 0 else (0, span)
-        part = pl.ds(first, count)
+    def sum_copy(s, k, part, way):
+        out, inp = sums[k][:2]
+        first, count = part_of(k, part)
+        span = pl.ds(first, count)
         return pltpu.make_async_remote_copy(
-            src_ref=out.at[s, way, part],
-            dst_ref=inp.at[s, way, part],
-            send_sem=sum_send.at[s, k, way],
-            recv_sem=sum_recv.at[s, k, way],
+            src_ref=out.at[s, way, span],
+            dst_ref=inp.at[s, way, span],
+            send_sem=sum_send.at[s, k, part, way],
+            recv_sem=sum_recv.at[s, k, part, way],
             device_id=((right if way == 0 else left), e),
             device_id_type=MESH,
         )
 
-    def sum_send_off(s, k, way):
-        copy = sum_copy(s, k, way)
+    def sum_send_off(s, k, part, way):
+        copy = sum_copy(s, k, part, way)
         copy.start()
         pending.append(copy)
 
     def sum_step(s, k):
-        out, inp, stage, span = sums[k]
+        out, inp, stage, _ = sums[k]
         if s == 0:
             block = partial_of(k, lax.rem(d + 4, NZ)).astype(BF)
             for way in (0, 1):
-                first, count = halves(k, way)
+                first, count = part_of(k, way)
                 out[0, way, first : first + count, :] = block[first : first + count, :]
-                sum_send_off(0, k, way)
+                sum_send_off(0, k, way, way)
             return
         if s == 4:
             block = partial_of(k, d)
+            for part in (0, 1):
+                first, count = part_of(k, part)
+                span = slice(first, first + count)
+                for way in (0, 1):
+                    sum_copy(3, k, part, way).wait_recv()
+                stage[span, :] = (
+                    block[span, :] + inp[3, 0, span, :].astype(F32) + inp[3, 1, span, :].astype(F32)
+                )
+            return
+        blocks = [
+            partial_of(k, lax.rem(d + 4 - s, NZ) if way == 0 else lax.rem(d + 4 + s, NZ))
+            for way in (0, 1)
+        ]
+        for n in (0, 1):
             for way in (0, 1):
-                sum_copy(3, k, way).wait_recv()
-            stage[...] = block + inp[3, 0].astype(F32) + inp[3, 1].astype(F32)
-            return
-        for way in (0, 1):
-            owner = lax.rem(d + 4 - s, NZ) if way == 0 else lax.rem(d + 4 + s, NZ)
-            block = partial_of(k, owner)
-            sum_copy(s - 1, k, way).wait_recv()
-            if s == 1:
-                first, count = halves(k, way)
-                span_in = slice(first, first + count)
-                out[s, way] = block.astype(BF)
-                out[s, way, span_in, :] = (
-                    block[span_in, :] + inp[0, way, span_in, :].astype(F32)
-                ).astype(BF)
-            else:
-                out[s, way] = (block + inp[s - 1, way].astype(F32)).astype(BF)
-            sum_send_off(s, k, way)
+                part = 1 - way if n == 0 else way
+                first, count = part_of(k, part)
+                span = slice(first, first + count)
+                value = blocks[way][span, :]
+                if s > 1 or n == 1:
+                    sum_copy(s - 1, k, part, way).wait_recv()
+                    value = value + inp[s - 1, way, span, :].astype(F32)
+                out[s, way, span, :] = value.astype(BF)
+                sum_send_off(s, k, part, way)
 
     sum_step(0, 1)
+    lax.fori_loop(0, SLOTS // 128, turn, 0)
     sum_step(0, 0)
 
     def route_tile(n, carry):
@@ -467,7 +520,7 @@
     sum_step(2, 1)
     landed(back_send, back_recv, back_send_sem, back_recv_sem)
     repack(back_recv, back_rows)
-    token_grad = jnp.dot(back_pick[...], back_rows[...], preferred_element_type=F32).astype(BF)
+    token_grad = contract_first(pick[0], back_rows[...]).astype(BF)
     sum_step(2, 0)
     sum_step(3, 1)
     sum_step(3, 0)
@@ -498,7 +551,7 @@
     dma = pltpu.SemaphoreType.DMA
     slots = (NE, CAP, 1024)
     flat = (SLOTS, 1024)
-    return pl.pallas_call(
+    results = pl.pallas_call(
         layer_kernel,
         out_shape=(
             jax.ShapeDtypeStruct((128, 4096), BF),
@@ -516,7 +569,6 @@
             pltpu.VMEM((128, 4096), BF),
             pltpu.VMEM((128, 1024), BF),
             pltpu.VMEM((2, SLOTS, 128), BF),
-            pltpu.VMEM((128, SLOTS), BF),
             pltpu.VMEM((128, 1024), F32),
             pltpu.VMEM(slots, BF),
             pltpu.VMEM(slots, BF),
@@ -524,6 +576,7 @@
             pltpu.VMEM((1024, SLOTS), BF),
             pltpu.VMEM(flat, BF),
             pltpu.VMEM((1408, SLOTS), BF),
+            pltpu.VMEM((SLOTS, 1408), F32),
             pltpu.VMEM((SLOTS, 1408), BF),
             pltpu.VMEM(slots, BF),
             pltpu.VMEM(slots, BF),
@@ -537,8 +590,8 @@
             pltpu.VMEM((176, 1024), F32),
             dma((NZ,)),
             dma((NZ,)),
-            dma((4, 2, 2)),
-            dma((4, 2, 2)),
+            dma((4, 2, 2, 2)),
+            dma((4, 2, 2, 2)),
             dma((2, 5, 4)),
             dma((2, 5, 4)),
             dma((2, 16)),
@@ -549,15 +602,43 @@
             dma((NE,)),
             dma((NE,)),
             dma((NE,)),
-            dma((4, 2, 2)),
-            dma((4, 2, 2)),
+            dma((4, 2, 2, 2)),
+            dma((4, 2, 2, 2)),
             dma((8,)),
         ],
         compiler_params=pltpu.CompilerParams(
             collective_id=0, has_side_effects=True, vmem_limit_bytes=60 * 1024 * 1024
         ),
         name="moe_backward",
-    )(tokens, proj, w1, w2, ids, gate, cot)
+    )(tokens, proj, w1, w2, ids.T, gate.T, cot)
+    return hand_out(*results)
+
+
+def hand_kernel(*refs):
+    sources, targets, held, sem = refs[:3], refs[3:6], refs[6:9], refs[9]
+    take = [pltpu.make_async_copy(sources[i], held[i], sem.at[0, i]) for i in range(3)]
+    give = [pltpu.make_async_copy(held[i], targets[i], sem.at[1, i]) for i in range(3)]
+    for copy in take:
+        copy.start()
+    for i in range(3):
+        take[i].wait()
+        give[i].start()
+    for copy in give:
+        copy.wait()
+
+
+def hand_out(*results):
+    anywhere = pl.BlockSpec(memory_space=pl.ANY)
+    return pl.pallas_call(
+        hand_kernel,
+        out_shape=tuple(jax.ShapeDtypeStruct(a.shape, a.dtype) for a in results),
+        in_specs=[anywhere] * 3,
+        out_specs=(anywhere,) * 3,
+        scratch_shapes=[pltpu.VMEM(a.shape, a.dtype) for a in results]
+        + [pltpu.SemaphoreType.DMA((2, 3))],
+        compiler_params=pltpu.CompilerParams(vmem_limit_bytes=60 * 1024 * 1024),
+        name="hand_out",
+    )(*results)
 
 
 def solution(mesh):

time: 162 us -> 147 us (0.907)
  Pallas kernels: 153 us -> 146 us
  local copies, waits for them, and re-layouts: 6.75 us -> 0 us
    pallas_call x1, Pallas kernels: 153 us -> 143 us  [layer(): pl.pallas_call(layer_kernel, out_shape=(jax.ShapeDtypeStruct((128, 4096),...]
    unnamed x11 -> x0, local copies, waits for them, and re-layouts: 6.75 us -> none
    pallas_call x0 -> x1, Pallas kernels: none -> 2.72 us  [hand_out(): pl.pallas_call(hand_kernel, out_shape=tuple((jax.ShapeDtypeStruct(a.shape...]
where the time goes in v3:
time: 147 us
  Pallas kernels  146 us (99%)
    pallas_call x1, Pallas kernels, layer(): pl.pallas_call(layer_kernel, out_shape=(jax.ShapeDtypeStruct((128, 4096),...  143 us

profile of v3, /device:TPU:2, one launch (start us, length us, event | category | flops | bytes accessed | tf_op | source)
XLA Modules:
  0.0 146.7 jit_solution(5398215276891507266)
XLA Ops:
  0.6 143.3 %moe_backward.1 = (bf16[128,4096]{1,0:T(8,128)(2,1)}, f32[1,128,1408]{2,1,0:T(8,128)}, f32[1,176,1024]{2,1,0:T(8,128)}) custom-call(bf16[128,4096]{1,0:T(8,128)(2,1)} %tokens_in.1, bf16[16,1024]{1,0:T(8,128)(2,1)} %proj_ref.1, bf16[1,128,1408]{2,1,0:T(8,128)(2,1)} %w1_ref.1, bf16[1,176,1024]{2,1,0:T(8,128)(2,1)} %w2_ref.1, s32[4,128]{1,0:T(4,128)} %bitcast.2, ...), custom_call_target="tpu_custom_call" | custom-call | tf_op jit(solution)/shard_map/moe_backward/pallas_call | solution.py:554
  144.0 2.7 %hand_out.1 = (bf16[128,4096]{1,0:T(8,128)(2,1)}, f32[1,128,1408]{2,1,0:T(8,128)}, f32[1,176,1024]{2,1,0:T(8,128)}) custom-call(bf16[128,4096]{1,0:T(8,128)(2,1)} %get-tuple-element.6.refs_0_, f32[1,128,1408]{2,1,0:T(8,128)} %get-tuple-element.7.refs_1_, f32[1,176,1024]{2,1,0:T(8,128)} %get-tuple-element.8.refs_2_), custom_call_target="tpu_custom_call" | custom-call | tf_op jit(solution)/shard_map/hand_out/pallas_call | solution.py:632

commit v4 on v3

--- a/solution.py
+++ b/solution.py
@@ -92,16 +92,14 @@
     rows_t,
     cots,
     hidden_t,
-    grad_hid,
+    active,
     grad_pre,
     back_send,
     back_recv,
-    back_rows,
     sum1_send,
     sum1_recv,
     sum2_send,
     sum2_recv,
-    gt_stage,
     g1_stage,
     g2_stage,
     zp_send,
@@ -147,12 +145,19 @@
     ]
     for copy in fetch:
         copy.start()
+    own = [pltpu.make_async_copy(proj_ref, col.at[2, e], local_sem.at[0])]
+    own[0].start()
     enter(d, e)
 
-    for i in range(1, NZ):
-        remote(proj_ref, col.at[d, e], zp_send.at[i], zp_recv.at[i], (lax.rem(d + i, NZ), e))
-    own = [pltpu.make_async_copy(proj_ref, col.at[d, e], local_sem.at[0])]
-    own[0].start()
+    own[0].wait()
+    for i in (1, 7, 2, 4, 3, 5, 6):
+        remote(
+            col.at[2, e],
+            col.at[(2 - i) % NZ, e],
+            zp_send.at[i],
+            zp_recv.at[i],
+            (lax.rem(d + i, NZ), e),
+        )
 
     weights = ((w1_ref, w1_out, 128), (w2_ref, w2_out, 176))
     def block_of(k, owner, first=0, count=None):
@@ -191,8 +196,6 @@
             arrived(block_of(k, owner, *part_of(k, part)), wz_recv.at[s, k, part, way])
             if s < 2 or (s == 2 and way == part):
                 ring_send(s + 1, k, part, way)
-
-    ring_first(1, 0)
 
     slot = lax.broadcasted_iota(jnp.int32, (SLOTS, 128), 0)
     of_expert = (slot * 2731) >> 16
@@ -213,7 +216,7 @@
     pick[1] = jnp.where(chosen, gates, 0.0).astype(BF)
     for copy in fetch:
         copy.wait()
-    ring_first(1, 1)
+    ring_first(0, 0)
 
     def pack(which, rows_ref, out):
         for j in range(4):
@@ -260,13 +263,12 @@
         pltpu.make_async_copy(buf.at[e], out.at[e], rsem.at[NE - 1]).wait()
 
     pack(1, cot_ref, send_cot)
-    ring_first(0, 0)
+    ring_first(0, 1)
     dispatch(send_cot, cot_out, cot_send_sem, cot_recv_sem, 0, 15)
-    ring_first(0, 1)
-
-    for i in range(1, NZ):
-        arrived(col.at[lax.rem(d - i + NZ, NZ), e], zp_recv.at[i])
-    own[0].wait()
+
+    def column(distances):
+        for i in distances:
+            arrived(col.at[(2 - i) % NZ, e], zp_recv.at[i])
 
     pos = ((x, y), (y, x))
 
@@ -297,13 +299,14 @@
             )
 
     for h in (0, 1):
+        column((3, 4, 5, 6) if h else (1, 2, 7))
         p, q = pos[h]
         spread(h, 0, device(h, p, q), 0)
-    for h in (0, 1):
-        p, q = pos[h]
         spread(h, 1, device(h, p, q), 1)
         share(h, device(h, p, q), 0)
-    ring_step(0, 1, 0)
+    ring_first(1, 0)
+    ring_first(1, 1)
+    ring_step(0, 0, 0)
     for h in (0, 1):
         p, q = pos[h]
         for w in (0, 1):
@@ -312,7 +315,7 @@
             spread(h, 0, who, 0, sub=w, way=w)
             spread(h, 1, who, 2 + w)
             share(h, who, 1 + w)
-    ring_step(0, 1, 1)
+    ring_step(0, 0, 1)
     for h in (0, 1):
         p, q = pos[h]
         who = device(h, p + 2, q)
@@ -320,7 +323,7 @@
             arrived(piece(h, who, w), ax_recv.at[h, 0, 2 + w])
         spread(h, 1, who, 4)
         share(h, who, 3)
-    ring_step(0, 0, 0)
+    ring_step(0, 1, 0)
 
     def second_stage(n):
         for h in (0, 1):
@@ -332,27 +335,22 @@
                 spread(h, 1, who, 1 + n, sub=w, way=w)
                 share(h, who, 4 + 3 * n + w)
 
-    def second_stage_far(n):
-        for h in (0, 1):
-            p, q = pos[h]
-            r = p + (0, -1, 1, 2)[n]
-            who = device(h, r, q + 2)
-            for w in (0, 1):
-                arrived(piece(h, who, w), ax_recv.at[h, 1 + n, 2 + w])
-            share(h, who, 6 + 3 * n)
+    def second_stage_far(h, n):
+        p, q = pos[h]
+        r = p + (0, -1, 1, 2)[n]
+        who = device(h, r, q + 2)
+        for w in (0, 1):
+            arrived(piece(h, who, w), ax_recv.at[h, 1 + n, 2 + w])
+        share(h, who, 6 + 3 * n)
 
     second_stage(0)
-    ring_step(0, 0, 1)
+    ring_step(0, 1, 1)
     second_stage(1)
     second_stage(2)
-    ring_step(1, 1, 0)
+    ring_step(1, 0, 0)
+    second_stage(3)
     dispatch(send_cot, cot_out, cot_send_sem, cot_recv_sem, 15)
-    second_stage(3)
-    ring_step(1, 1, 1)
-
-    for n in range(4):
-        second_stage_far(n)
-    ring_step(1, 0, 0)
+    ring_step(1, 0, 1)
 
     def other(h, p, q):
         p, q = lax.rem(p + 2 * NX, NX), lax.rem(q + 2 * NX, NX)
@@ -362,79 +360,113 @@
     for n in range(4):
         r = (0, -1, 1, 2)[n]
         order += [(r, -1), (r, 1), (r, 2)]
-    for h in (0, 1):
+
+    def other_core(h):
         p, q = pos[h]
         for n, (a, b) in enumerate(order):
             arrived(piece(h, other(h, p + a, q + b)), mate_recv.at[h, n])
 
+    def half(n):
+        return slice(512 * n, 512 * (n + 1))
+
+    def plane(r):
+        return pl.ds(pl.multiple_of(lax.rem(d + r + NZ - 2, NZ) * 512, 512), 512)
+
+    def latent_sum(n, h):
+        def step(r, carry):
+            block = col[r, :, :, half(n)].reshape(512, 512)
+            acc[n] += jnp.dot(tokens_ref[:, plane(r)], block, preferred_element_type=F32)
+            return carry
+
+        lax.fori_loop(4 * h, 4 * h + 4, step, 0)
+
+    def latent_half(n):
+        latent_sum(n, 1)
+        latent = acc[n].astype(BF)
+        for j in range(4):
+            block = jnp.dot(
+                pick[0, 192 * j : 192 * (j + 1), :], latent, preferred_element_type=F32
+            )
+            for i in range(8):
+                send_lat[n, 8 * j + i] = block[CAP * i : CAP * (i + 1), :].astype(BF)
+        dispatch(
+            send_lat.at[n], lat_out.at[n], lat_send_sem.at[n], lat_recv_sem.at[n]
+        )
+
     acc[...] = jnp.zeros_like(acc)
-
-    def latent_step(j, carry):
-        block = col[j].reshape(512, 1024)
-        acc[...] += jnp.dot(
-            tokens_ref[:, pl.ds(pl.multiple_of(j * 512, 512), 512)], block, preferred_element_type=F32
-        )
-        return carry
-
-    lax.fori_loop(0, NZ, latent_step, 0)
-    ring_step(1, 0, 1)
-    latent = acc[...].astype(BF)
-    for j in range(4):
-        block = jnp.dot(pick[0, 192 * j : 192 * (j + 1), :], latent, preferred_element_type=F32)
-        for i in range(8):
-            send_lat[8 * j + i] = block[CAP * i : CAP * (i + 1), :].astype(BF)
-    dispatch(send_lat, lat_out, lat_send_sem, lat_recv_sem)
-
-    def repack(buf, out):
+    for n in range(4):
+        second_stage_far(0, n)
+    other_core(0)
+    for n in (0, 1):
+        latent_sum(n, 0)
+    for n in range(4):
+        second_stage_far(1, n)
+    ring_step(1, 1, 0)
+    other_core(1)
+    latent_half(0)
+    ring_step(1, 1, 1)
+    latent_half(1)
+    ring_step(2, 0, 0)
+    ring_step(2, 0, 1)
+
+    def repack(buf, out, columns=slice(None)):
         def go(j, carry):
             pair = jnp.concatenate([buf[2 * j].astype(F32), buf[2 * j + 1].astype(F32)], axis=0)
-            out[pl.ds(pl.multiple_of(j * 48, 16), 48), :] = pair.astype(BF)
+            out[pl.ds(pl.multiple_of(j * 48, 16), 48), columns] = pair.astype(BF)
             return carry
 
         lax.fori_loop(0, NE // 2, go, 0)
 
+    landed(send_cot, cot_out, cot_send_sem, cot_recv_sem)
+    repack(cot_out, cots)
     ring_step(2, 1, 0)
     ring_step(2, 1, 1)
-    landed(send_cot, cot_out, cot_send_sem, cot_recv_sem)
-    ring_step(2, 0, 0)
-    repack(cot_out, cots)
-    ring_step(2, 0, 1)
-    ring_step(3, 1, 0)
-    ring_step(3, 1, 1)
-    own[2].wait()
-
-    def tiles(tile):
-        def go(j, carry):
-            tile(j * 256, 256)
-            return carry
-
-        lax.fori_loop(0, 5, go, 0)
-        tile(1280, 128)
-
-    def cot_tile(start, width):
-        part = pl.ds(pl.multiple_of(start, 128), width)
-        grad_hid[:, part] = contract_last(cots[...], w2_out[part, :])
-
-    tiles(cot_tile)
     ring_step(3, 0, 0)
     ring_step(3, 0, 1)
     own[1].wait()
-    landed(send_lat, lat_out, lat_send_sem, lat_recv_sem)
-    repack(lat_out, rows)
-
-    def hidden_tile(start, width):
-        part = pl.ds(pl.multiple_of(start, 128), width)
-        preact = jnp.dot(rows[...], w1_out[:, part], preferred_element_type=F32)
-        active = jnp.maximum(preact, 0.0)
-        hidden_t[part, :] = (active * active).astype(BF).T
-        grad_pre[:, part] = (grad_hid[:, part] * 2.0 * active).astype(BF)
-
+
+    def tiles(tile):
+        def go(j, carry):
+            tile(pl.ds(pl.multiple_of(j * 256, 256), 256))
+            return carry
+
+        lax.fori_loop(0, 5, go, 0)
+        tile(slice(1280, 1408))
+
+    def latents_in(n):
+        landed(send_lat.at[n], lat_out.at[n], lat_send_sem.at[n], lat_recv_sem.at[n])
+        repack(lat_out.at[n], rows, half(n))
+
+    def turn(n):
+        def go(j, carry):
+            part = pl.ds(pl.multiple_of(j * 128, 128), 128)
+            rows_t[half(n), part] = rows[part, half(n)].T
+            return carry
+
+        lax.fori_loop(0, SLOTS // 128, go, 0)
+
+    def preact_tile(part):
+        active[:, part] = jnp.dot(
+            rows[:, half(0)], w1_out[half(0), part], preferred_element_type=F32
+        )
+
+    def hidden_tile(part):
+        preact = active[:, part] + jnp.dot(
+            rows[:, half(1)], w1_out[half(1), part], preferred_element_type=F32
+        )
+        positive = jnp.maximum(preact, 0.0)
+        active[:, part] = positive
+        hidden_t[part, :] = (positive * positive).astype(BF).T
+
+    def grad_tile(part):
+        grad_hidden = contract_last(cots[...], w2_out[part, :])
+        grad_pre[:, part] = (grad_hidden * 2.0 * active[:, part]).astype(BF)
+
+    latents_in(0)
+    tiles(preact_tile)
+    turn(0)
+    latents_in(1)
     tiles(hidden_tile)
-
-    def turn(j, carry):
-        part = pl.ds(pl.multiple_of(j * 128, 128), 128)
-        rows_t[:, part] = rows[part, :].T
-        return carry
 
     sums = (
         (sum1_send, sum1_recv, g1_stage, 128),
@@ -466,45 +498,69 @@
         copy.start()
         pending.append(copy)
 
-    def sum_step(s, k):
+    def sum_first(k):
+        out = sums[k][0]
+        block = partial_of(k, lax.rem(d + 4, NZ)).astype(BF)
+        for way in (0, 1):
+            first, count = part_of(k, way)
+            out[0, way, first : first + count, :] = block[first : first + count, :]
+            sum_send_off(0, k, way, way)
+
+    def prepare(s, k):
+        out, _, stage, _ = sums[k]
+        if s == 4:
+            stage[...] = partial_of(k, d)
+            return
+        for way in (0, 1):
+            owner = lax.rem(d + 4 - s, NZ) if way == 0 else lax.rem(d + 4 + s, NZ)
+            out[s, way] = partial_of(k, owner).astype(BF)
+
+    def finish(s, k):
         out, inp, stage, _ = sums[k]
-        if s == 0:
-            block = partial_of(k, lax.rem(d + 4, NZ)).astype(BF)
-            for way in (0, 1):
-                first, count = part_of(k, way)
-                out[0, way, first : first + count, :] = block[first : first + count, :]
-                sum_send_off(0, k, way, way)
-            return
-        if s == 4:
-            block = partial_of(k, d)
-            for part in (0, 1):
-                first, count = part_of(k, part)
-                span = slice(first, first + count)
-                for way in (0, 1):
-                    sum_copy(3, k, part, way).wait_recv()
-                stage[span, :] = (
-                    block[span, :] + inp[3, 0, span, :].astype(F32) + inp[3, 1, span, :].astype(F32)
-                )
-            return
-        blocks = [
-            partial_of(k, lax.rem(d + 4 - s, NZ) if way == 0 else lax.rem(d + 4 + s, NZ))
-            for way in (0, 1)
-        ]
         for n in (0, 1):
             for way in (0, 1):
                 part = 1 - way if n == 0 else way
                 first, count = part_of(k, part)
                 span = slice(first, first + count)
-                value = blocks[way][span, :]
-                if s > 1 or n == 1:
-                    sum_copy(s - 1, k, part, way).wait_recv()
-                    value = value + inp[s - 1, way, span, :].astype(F32)
-                out[s, way, span, :] = value.astype(BF)
-                sum_send_off(s, k, part, way)
-
-    sum_step(0, 1)
-    lax.fori_loop(0, SLOTS // 128, turn, 0)
-    sum_step(0, 0)
+                sum_copy(s - 1, k, part, way).wait_recv()
+                more = inp[s - 1, way, span, :].astype(F32)
+                if s == 4:
+                    stage[span, :] += more
+                else:
+                    out[s, way, span, :] = (out[s, way, span, :].astype(F32) + more).astype(BF)
+                    sum_send_off(s, k, part, way)
+
+    def sum_start(k):
+        out, inp, stage, _ = sums[k]
+        sum_first(k)
+        for way in (0, 1):
+            block = partial_of(k, lax.rem(d + 3, NZ) if way == 0 else lax.rem(d + 5, NZ))
+            first, count = part_of(k, 1 - way)
+            span = slice(first, first + count)
+            out[1, way, span, :] = block[span, :].astype(BF)
+            sum_send_off(1, k, 1 - way, way)
+            first, count = part_of(k, way)
+            span = slice(first, first + count)
+            stage[span, :] = block[span, :]
+
+    def sum_second(k):
+        out, inp, stage, _ = sums[k]
+        for way in (0, 1):
+            first, count = part_of(k, way)
+            span = slice(first, first + count)
+            sum_copy(0, k, way, way).wait_recv()
+            value = stage[span, :] + inp[0, way, span, :].astype(F32)
+            out[1, way, span, :] = value.astype(BF)
+            sum_send_off(1, k, way, way)
+
+    sum_start(1)
+    ring_step(3, 1, 0)
+    ring_step(3, 1, 1)
+    own[2].wait()
+    tiles(grad_tile)
+    turn(1)
+    sum_start(0)
+    sum_second(1)
 
     def route_tile(n, carry):
         part = pl.ds(pl.multiple_of(n * 256, 256), 256)
@@ -515,31 +571,39 @@
 
     lax.fori_loop(0, 4, route_tile, 0)
     dispatch(back_send, back_recv, back_send_sem, back_recv_sem)
-    sum_step(1, 1)
-    sum_step(1, 0)
-    sum_step(2, 1)
+    prepare(2, 1)
+    sum_second(0)
+    prepare(2, 0)
+    finish(2, 1)
+    prepare(3, 1)
+    finish(2, 0)
+    prepare(3, 0)
+    prepare(4, 1)
+    finish(3, 1)
+    prepare(4, 0)
+    finish(3, 0)
+    early = len(pending) - 8
+    for copy in pending[:early]:
+        copy.wait_send()
     landed(back_send, back_recv, back_send_sem, back_recv_sem)
-    repack(back_recv, back_rows)
-    token_grad = contract_first(pick[0], back_rows[...]).astype(BF)
-    sum_step(2, 0)
-    sum_step(3, 1)
-    sum_step(3, 0)
+    repack(back_recv, rows)
+    token_grad = contract_first(pick[0], rows[...]).astype(BF)
 
     def token_tile(j, carry):
         block = contract_last(token_grad, col[j].reshape(512, 1024))
-        gt_stage[:, pl.ds(pl.multiple_of(j * 512, 512), 512)] = block.astype(BF)
+        tokens_ref[:, plane(j)] = block.astype(BF)
         return carry
 
     lax.fori_loop(0, NZ, token_tile, 0)
-    leave = [pltpu.make_async_copy(gt_stage, gt_out, local_sem.at[5])]
+    leave = [pltpu.make_async_copy(tokens_ref, gt_out, local_sem.at[5])]
     leave[0].start()
-    sum_step(4, 1)
+    finish(4, 1)
     leave.append(pltpu.make_async_copy(g2_stage, g2_out.at[0], local_sem.at[6]))
     leave[1].start()
-    sum_step(4, 0)
+    finish(4, 0)
     leave.append(pltpu.make_async_copy(g1_stage, g1_out.at[0], local_sem.at[7]))
     leave[2].start()
-    for copy in pending:
+    for copy in pending[early:]:
         copy.wait_send()
     for copy in leave:
         copy.wait()
@@ -550,6 +614,7 @@
     vmem = pl.BlockSpec(memory_space=pltpu.VMEM)
     dma = pltpu.SemaphoreType.DMA
     slots = (NE, CAP, 1024)
+    halves = (2, NE, CAP, 512)
     flat = (SLOTS, 1024)
     results = pl.pallas_call(
         layer_kernel,
@@ -564,13 +629,13 @@
             pltpu.VMEM((NZ, NE, 16, 1024), BF),
             pltpu.VMEM((1024, 1408), BF),
             pltpu.VMEM((1408, 1024), BF),
-            pltpu.VMEM(slots, BF),
+            pltpu.VMEM(halves, BF),
             pltpu.VMEM(slots, BF),
             pltpu.VMEM((128, 4096), BF),
             pltpu.VMEM((128, 1024), BF),
             pltpu.VMEM((2, SLOTS, 128), BF),
-            pltpu.VMEM((128, 1024), F32),
-            pltpu.VMEM(slots, BF),
+            pltpu.VMEM((2, 128, 512), F32),
+            pltpu.VMEM(halves, BF),
             pltpu.VMEM(slots, BF),
             pltpu.VMEM(flat, BF),
             pltpu.VMEM((1024, SLOTS), BF),
@@ -580,12 +645,10 @@
             pltpu.VMEM((SLOTS, 1408), BF),
             pltpu.VMEM(slots, BF),
             pltpu.VMEM(slots, BF),
-            pltpu.VMEM(flat, BF),
             pltpu.VMEM((4, 2, 128, 1408), BF),
             pltpu.VMEM((4, 2, 128, 1408), BF),
             pltpu.VMEM((4, 2, 176, 1024), BF),
             pltpu.VMEM((4, 2, 176, 1024), BF),
-            pltpu.VMEM((128, 4096), BF),
             pltpu.VMEM((128, 1408), F32),
             pltpu.VMEM((176, 1024), F32),
             dma((NZ,)),
@@ -596,8 +659,8 @@
             dma((2, 5, 4)),
             dma((2, 16)),
             dma((2, 16)),
-            dma((NE,)),
-            dma((NE,)),
+            dma((2, NE)),
+            dma((2, NE)),
             dma((NE,)),
             dma((NE,)),
             dma((NE,)),

time: 147 us -> 142 us (0.966); the launches traced: 147 us -> 140 us
  Pallas kernels: 146 us -> 139 us
    pallas_call x1, Pallas kernels: 143 us -> 136 us  [layer(): pl.pallas_call(layer_kernel, out_shape=(jax.ShapeDtypeStruct((128, 4096),...]
where the time goes in v4:
time: 142 us; the launch traced here: 140 us
  Pallas kernels  139 us (98%)
    pallas_call x1, Pallas kernels, layer(): pl.pallas_call(layer_kernel, out_shape=(jax.ShapeDtypeStruct((128, 4096),...  136 us

profile of v4, /device:TPU:2, one launch (start us, length us, event | category | flops | bytes accessed | tf_op | source)
XLA Modules:
  0.0 139.7 jit_solution(11229400750960312277)
XLA Ops:
  0.6 136.2 %moe_backward.1 = (bf16[128,4096]{1,0:T(8,128)(2,1)}, f32[1,128,1408]{2,1,0:T(8,128)}, f32[1,176,1024]{2,1,0:T(8,128)}) custom-call(bf16[128,4096]{1,0:T(8,128)(2,1)} %tokens_in.1, bf16[16,1024]{1,0:T(8,128)(2,1)} %proj_ref.1, bf16[1,128,1408]{2,1,0:T(8,128)(2,1)} %w1_ref.1, bf16[1,176,1024]{2,1,0:T(8,128)(2,1)} %w2_ref.1, s32[4,128]{1,0:T(4,128)} %bitcast.2, ...), custom_call_target="tpu_custom_call" | custom-call | tf_op jit(solution)/shard_map/moe_backward/pallas_call | solution.py:619
  136.8 2.7 %hand_out.1 = (bf16[128,4096]{1,0:T(8,128)(2,1)}, f32[1,128,1408]{2,1,0:T(8,128)}, f32[1,176,1024]{2,1,0:T(8,128)}) custom-call(bf16[128,4096]{1,0:T(8,128)(2,1)} %get-tuple-element.6.refs_0_, f32[1,128,1408]{2,1,0:T(8,128)} %get-tuple-element.7.refs_1_, f32[1,176,1024]{2,1,0:T(8,128)} %get-tuple-element.8.refs_2_), custom_call_target="tpu_custom_call" | custom-call | tf_op jit(solution)/shard_map/hand_out/pallas_call | solution.py:695

commit v5 on v4

--- a/solution.py
+++ b/solution.py
@@ -14,6 +14,7 @@
 NE = 32
 CAP = 24
 SLOTS = NE * CAP
+DEPTH = 4
 FAR_FIRST = (
     (2, 2),
     (2, 1),
@@ -163,7 +164,9 @@
     def block_of(k, owner, first=0, count=None):
         span = weights[k][2]
         start = pl.multiple_of(owner * span + first, 16)
-        return weights[k][1].at[pl.ds(start, span if count is None else count)]
+        held = weights[k][1]
+        part = pl.ds(start, span if count is None else count)
+        return held.at[part, pl.ds(0, 1408)] if k == 0 else held.at[part]
 
     for k, (src, dst, _) in enumerate(weights):
         copy = pltpu.make_async_copy(src.at[0], block_of(k, d), local_sem.at[1 + k])
@@ -394,6 +397,8 @@
         )
 
     acc[...] = jnp.zeros_like(acc)
+    w1_out[:, 1408:] = jnp.zeros((1024, 128), BF)
+    active[:, 1408:] = jnp.zeros((SLOTS, 128), F32)
     for n in range(4):
         second_stage_far(0, n)
     other_core(0)
@@ -466,7 +471,14 @@
     tiles(preact_tile)
     turn(0)
     latents_in(1)
-    tiles(hidden_tile)
+    foremost = (176 * lax.rem(d + 4, NZ)) // 256
+
+    def hidden_turn(j, carry):
+        start = lax.rem(foremost + j, 6) * 256
+        hidden_tile(pl.ds(pl.multiple_of(start, 256), 256))
+        return carry
+
+    lax.fori_loop(0, 2, hidden_turn, 0)
 
     sums = (
         (sum1_send, sum1_recv, g1_stage, 128),
@@ -493,97 +505,87 @@
             device_id_type=MESH,
         )
 
+    flying = ([], [])
+
     def sum_send_off(s, k, part, way):
+        if len(flying[way]) == DEPTH:
+            flying[way].pop(0).wait_send()
         copy = sum_copy(s, k, part, way)
         copy.start()
-        pending.append(copy)
-
-    def sum_first(k):
-        out = sums[k][0]
-        block = partial_of(k, lax.rem(d + 4, NZ)).astype(BF)
-        for way in (0, 1):
-            first, count = part_of(k, way)
-            out[0, way, first : first + count, :] = block[first : first + count, :]
-            sum_send_off(0, k, way, way)
+        flying[way].append(copy)
 
     def prepare(s, k):
         out, _, stage, _ = sums[k]
         if s == 4:
             stage[...] = partial_of(k, d)
             return
+        if s == 0:
+            block = partial_of(k, lax.rem(d + 4, NZ)).astype(BF)
+            for way in (0, 1):
+                first, count = part_of(k, way)
+                out[0, way, first : first + count, :] = block[first : first + count, :]
+            return
         for way in (0, 1):
             owner = lax.rem(d + 4 - s, NZ) if way == 0 else lax.rem(d + 4 + s, NZ)
             out[s, way] = partial_of(k, owner).astype(BF)
 
-    def finish(s, k):
+    def push(s, k, late):
         out, inp, stage, _ = sums[k]
-        for n in (0, 1):
-            for way in (0, 1):
-                part = 1 - way if n == 0 else way
-                first, count = part_of(k, part)
-                span = slice(first, first + count)
+        for way in (0, 1):
+            part = way if late else 1 - way
+            first, count = part_of(k, part)
+            span = slice(first, first + count)
+            if s > 1 or (s == 1 and late):
                 sum_copy(s - 1, k, part, way).wait_recv()
                 more = inp[s - 1, way, span, :].astype(F32)
                 if s == 4:
                     stage[span, :] += more
                 else:
                     out[s, way, span, :] = (out[s, way, span, :].astype(F32) + more).astype(BF)
-                    sum_send_off(s, k, part, way)
-
-    def sum_start(k):
-        out, inp, stage, _ = sums[k]
-        sum_first(k)
-        for way in (0, 1):
-            block = partial_of(k, lax.rem(d + 3, NZ) if way == 0 else lax.rem(d + 5, NZ))
-            first, count = part_of(k, 1 - way)
-            span = slice(first, first + count)
-            out[1, way, span, :] = block[span, :].astype(BF)
-            sum_send_off(1, k, 1 - way, way)
-            first, count = part_of(k, way)
-            span = slice(first, first + count)
-            stage[span, :] = block[span, :]
-
-    def sum_second(k):
-        out, inp, stage, _ = sums[k]
-        for way in (0, 1):
-            first, count = part_of(k, way)
-            span = slice(first, first + count)
-            sum_copy(0, k, way, way).wait_recv()
-            value = stage[span, :] + inp[0, way, span, :].astype(F32)
-            out[1, way, span, :] = value.astype(BF)
-            sum_send_off(1, k, way, way)
-
-    sum_start(1)
+            if s < 4:
+                sum_send_off(s, k, part, way)
+
+    prepare(0, 1)
+    push(0, 1, True)
+    lax.fori_loop(2, 6, hidden_turn, 0)
+    prepare(1, 1)
+    push(1, 1, False)
     ring_step(3, 1, 0)
     ring_step(3, 1, 1)
     own[2].wait()
     tiles(grad_tile)
     turn(1)
-    sum_start(0)
-    sum_second(1)
+    prepare(0, 0)
+    push(0, 0, True)
+    prepare(1, 0)
+    push(1, 0, False)
+    prepare(2, 1)
+    push(1, 1, True)
+    push(2, 1, False)
 
     def route_tile(n, carry):
         part = pl.ds(pl.multiple_of(n * 256, 256), 256)
-        block = contract_last(grad_pre[...], w1_out[part, :])
+        block = contract_last(grad_pre[...], w1_out[part, :1408])
         for i in range(NE):
             back_send[i, :, part] = block[CAP * i : CAP * (i + 1), :].astype(BF)
         return carry
 
     lax.fori_loop(0, 4, route_tile, 0)
     dispatch(back_send, back_recv, back_send_sem, back_recv_sem)
-    prepare(2, 1)
-    sum_second(0)
     prepare(2, 0)
-    finish(2, 1)
+    push(1, 0, True)
+    push(2, 0, False)
     prepare(3, 1)
-    finish(2, 0)
+    push(2, 1, True)
+    push(3, 1, False)
     prepare(3, 0)
+    push(2, 0, True)
+    push(3, 0, False)
     prepare(4, 1)
-    finish(3, 1)
     prepare(4, 0)
-    finish(3, 0)
-    early = len(pending) - 8
-    for copy in pending[:early]:
+    push(3, 1, True)
+    push(3, 0, True)
+    for copy in pending:
         copy.wait_send()
     landed(back_send, back_recv, back_send_sem, back_recv_sem)
     repack(back_recv, rows)
@@ -597,13 +599,15 @@
     lax.fori_loop(0, NZ, token_tile, 0)
     leave = [pltpu.make_async_copy(tokens_ref, gt_out, local_sem.at[5])]
     leave[0].start()
-    finish(4, 1)
+    push(4, 1, False)
+    push(4, 1, True)
     leave.append(pltpu.make_async_copy(g2_stage, g2_out.at[0], local_sem.at[6]))
     leave[1].start()
-    finish(4, 0)
+    push(4, 0, False)
+    push(4, 0, True)
     leave.append(pltpu.make_async_copy(g1_stage, g1_out.at[0], local_sem.at[7]))
     leave[2].start()
-    for copy in pending[early:]:
+    for copy in flying[0] + flying[1]:
         copy.wait_send()
     for copy in leave:
         copy.wait()
@@ -627,7 +631,7 @@
         out_specs=(anywhere,) * 3,
         scratch_shapes=[
             pltpu.VMEM((NZ, NE, 16, 1024), BF),
-            pltpu.VMEM((1024, 1408), BF),
+            pltpu.VMEM((1024, 1536), BF),
             pltpu.VMEM((1408, 1024), BF),
             pltpu.VMEM(halves, BF),
             pltpu.VMEM(slots, BF),
@@ -640,8 +644,8 @@
             pltpu.VMEM(flat, BF),
             pltpu.VMEM((1024, SLOTS), BF),
             pltpu.VMEM(flat, BF),
-            pltpu.VMEM((1408, SLOTS), BF),
-            pltpu.VMEM((SLOTS, 1408), F32),
+            pltpu.VMEM((1536, SLOTS), BF),
+            pltpu.VMEM((SLOTS, 1536), F32),
             pltpu.VMEM((SLOTS, 1408), BF),
             pltpu.VMEM(slots, BF),
             pltpu.VMEM(slots, BF),
@@ -679,13 +683,26 @@
 
 def hand_kernel(*refs):
     sources, targets, held, sem = refs[:3], refs[3:6], refs[6:9], refs[9]
-    take = [pltpu.make_async_copy(sources[i], held[i], sem.at[0, i]) for i in range(3)]
-    give = [pltpu.make_async_copy(held[i], targets[i], sem.at[1, i]) for i in range(3)]
+
+    def piece(ref, half):
+        rows = ref.shape[-2] // 2
+        part = pl.ds(half * rows, rows)
+        return ref.at[part] if len(ref.shape) == 2 else ref.at[0, part]
+
+    each = [(i, half) for i in range(3) for half in (0, 1)]
+    take = [
+        pltpu.make_async_copy(piece(sources[i], h), piece(held[i], h), sem.at[0, i, h])
+        for i, h in each
+    ]
+    give = [
+        pltpu.make_async_copy(piece(held[i], h), piece(targets[i], h), sem.at[1, i, h])
+        for i, h in each
+    ]
     for copy in take:
         copy.start()
-    for i in range(3):
-        take[i].wait()
-        give[i].start()
+    for came, goes in zip(take, give):
+        came.wait()
+        goes.start()
     for copy in give:
         copy.wait()
 
@@ -698,7 +715,7 @@
         in_specs=[anywhere] * 3,
         out_specs=(anywhere,) * 3,
         scratch_shapes=[pltpu.VMEM(a.shape, a.dtype) for a in results]
-        + [pltpu.SemaphoreType.DMA((2, 3))],
+        + [pltpu.SemaphoreType.DMA((2, 3, 2))],
         compiler_params=pltpu.CompilerParams(vmem_limit_bytes=60 * 1024 * 1024),
         name="hand_out",
     )(*results)

time: 142 us -> 140 us (0.986)
  Pallas kernels: 139 us -> 137 us
    pallas_call x1, Pallas kernels: 136 us -> 135 us  [layer(): pl.pallas_call(layer_kernel, out_shape=(jax.ShapeDtypeStruct((128, 4096),...]
where the time goes in v5:
time: 140 us; the launch traced here: 138 us
  Pallas kernels  137 us (98%)
    pallas_call x1, Pallas kernels, layer(): pl.pallas_call(layer_kernel, out_shape=(jax.ShapeDtypeStruct((128, 4096),...  135 us

profile of v5, /device:TPU:2, one launch (start us, length us, event | category | flops | bytes accessed | tf_op | source)
XLA Modules:
  0.0 138.0 jit_solution(2415433802712287934)
XLA Ops:
  0.6 134.6 %moe_backward.1 = (bf16[128,4096]{1,0:T(8,128)(2,1)}, f32[1,128,1408]{2,1,0:T(8,128)}, f32[1,176,1024]{2,1,0:T(8,128)}) custom-call(bf16[128,4096]{1,0:T(8,128)(2,1)} %tokens_in.1, bf16[16,1024]{1,0:T(8,128)(2,1)} %proj_ref.1, bf16[1,128,1408]{2,1,0:T(8,128)(2,1)} %w1_ref.1, bf16[1,176,1024]{2,1,0:T(8,128)(2,1)} %w2_ref.1, s32[4,128]{1,0:T(4,128)} %bitcast.2, ...), custom_call_target="tpu_custom_call" | custom-call | tf_op jit(solution)/shard_map/moe_backward/pallas_call | solution.py:623
  135.3 2.6 %hand_out.1 = (bf16[128,4096]{1,0:T(8,128)(2,1)}, f32[1,128,1408]{2,1,0:T(8,128)}, f32[1,176,1024]{2,1,0:T(8,128)}) custom-call(bf16[128,4096]{1,0:T(8,128)(2,1)} %get-tuple-element.6.refs_0_, f32[1,128,1408]{2,1,0:T(8,128)} %get-tuple-element.7.refs_1_, f32[1,176,1024]{2,1,0:T(8,128)} %get-tuple-element.8.refs_2_), custom_call_target="tpu_custom_call" | custom-call | tf_op jit(solution)/shard_map/hand_out/pallas_call | solution.py:712

commit v6 on v5

--- a/solution.py
+++ b/solution.py
@@ -268,6 +268,9 @@
     pack(1, cot_ref, send_cot)
     ring_first(0, 1)
     dispatch(send_cot, cot_out, cot_send_sem, cot_recv_sem, 0, 15)
+    acc[...] = jnp.zeros_like(acc)
+    w1_out[:, 1408:] = jnp.zeros((1024, 128), BF)
+    active[:, 1408:] = jnp.zeros((SLOTS, 128), F32)
 
     def column(distances):
         for i in distances:
@@ -396,9 +399,6 @@
             send_lat.at[n], lat_out.at[n], lat_send_sem.at[n], lat_recv_sem.at[n]
         )
 
-    acc[...] = jnp.zeros_like(acc)
-    w1_out[:, 1408:] = jnp.zeros((1024, 128), BF)
-    active[:, 1408:] = jnp.zeros((SLOTS, 128), F32)
     for n in range(4):
         second_stage_far(0, n)
     other_core(0)
@@ -422,8 +422,6 @@
 
         lax.fori_loop(0, NE // 2, go, 0)
 
-    landed(send_cot, cot_out, cot_send_sem, cot_recv_sem)
-    repack(cot_out, cots)
     ring_step(2, 1, 0)
     ring_step(2, 1, 1)
     ring_step(3, 0, 0)
@@ -470,6 +468,8 @@
     latents_in(0)
     tiles(preact_tile)
     turn(0)
+    landed(send_cot, cot_out, cot_send_sem, cot_recv_sem)
+    repack(cot_out, cots)
     latents_in(1)
     foremost = (176 * lax.rem(d + 4, NZ)) // 256
 

time: 140 us -> 140 us (level)
  no operation moved by 1% of the time
where the time goes in v6:
time: 140 us; the launch traced here: 138 us
  Pallas kernels  137 us (98%)
    pallas_call x1, Pallas kernels, layer(): pl.pallas_call(layer_kernel, out_shape=(jax.ShapeDtypeStruct((128, 4096),...  135 us

profile of v6, /device:TPU:2, one launch (start us, length us, event | category | flops | bytes accessed | tf_op | source)
XLA Modules:
  0.0 138.2 jit_solution(3631003130967951096)
XLA Ops:
  0.6 134.8 %moe_backward.1 = (bf16[128,4096]{1,0:T(8,128)(2,1)}, f32[1,128,1408]{2,1,0:T(8,128)}, f32[1,176,1024]{2,1,0:T(8,128)}) custom-call(bf16[128,4096]{1,0:T(8,128)(2,1)} %tokens_in.1, bf16[16,1024]{1,0:T(8,128)(2,1)} %proj_ref.1, bf16[1,128,1408]{2,1,0:T(8,128)(2,1)} %w1_ref.1, bf16[1,176,1024]{2,1,0:T(8,128)(2,1)} %w2_ref.1, s32[4,128]{1,0:T(4,128)} %bitcast.2, ...), custom_call_target="tpu_custom_call" | custom-call | tf_op jit(solution)/shard_map/moe_backward/pallas_call | solution.py:623
  135.5 2.6 %hand_out.1 = (bf16[128,4096]{1,0:T(8,128)(2,1)}, f32[1,128,1408]{2,1,0:T(8,128)}, f32[1,176,1024]{2,1,0:T(8,128)}) custom-call(bf16[128,4096]{1,0:T(8,128)(2,1)} %get-tuple-element.6.refs_0_, f32[1,128,1408]{2,1,0:T(8,128)} %get-tuple-element.7.refs_1_, f32[1,176,1024]{2,1,0:T(8,128)} %get-tuple-element.8.refs_2_), custom_call_target="tpu_custom_call" | custom-call | tf_op jit(solution)/shard_map/hand_out/pallas_call | solution.py:712
